TPU v7x, 32 devices: a whole 2x2x4 slice. The times are simulated.
32 devices in a mesh: band: 16 (over z, x, core), lev: 2 (over y).
Axes of the slice: x: 2, y: 2, z: 4, core: 2. Of those that a mesh axis runs over, the one named last changes fastest.
Arguments:
- air_fourier_coefficients: float32 [4, 16, 1280, 128], P('lev', None, 'band'), may hold values from -6 to 6
- quadrature_factor: float32 [1280], P('band'), may hold values from 0.5 to 1.5
- associated_polynomial_table: bfloat16 [64, 1280, 1280], P('band'), may hold values from -6 to 6
- east_west_harmonic: int32 [64], replicated, may hold values from 0 to 1279, as said below
- boundary_diffusion: float32 [4, 16, 16, 1280], P('lev', None, None, 'band'), may hold values from -0.25 to 0.25
- bulk_transfer_coefficient: float32 [4, 1280], P('lev', 'band'), may hold values from 0.1 to 1
- skin_heat_earlier: float32 [12, 4, 1280, 128], P(None, 'lev', 'band'), may hold values from -6 to 6
- sea_boundary_values: float32 [4, 512, 1440], P('lev', 'band'), may hold values from -6 to 6
- sea_damping_speed: float32 [4, 512, 1440], P('lev', 'band'), may hold values from 0.02 to 2
- sea_coupling_matrix: float32 [4, 4], replicated, may hold values from -1.75 to 1.75
- patch_active_entries: int32 [16], P('band'), may hold values from 8 to 32, as said below
- sea_southern_parallel: int32 [512], P('band'), may hold values from 0 to 1278, as said below
- sea_northern_share: float32 [512], P('band'), may hold values from 0 to 1
- air_paired_cells: int32 [2, 1280], P(None, 'band'), may hold values from 0 to 511, as said below
- air_second_share: float32 [1280], P('band'), may hold values from 0 to 1
Outputs:
- air_coefficients_end: float32 [4, 16, 1280, 128], P('lev', None, 'band')
- sea_values_end: float32 [4, 512, 1440], P('lev', 'band')
- skin_heat_newest: float32 [12, 4, 1280, 128], P(None, 'lev', 'band')
Inputs may be any that keep to these rules, and one draw needn't show every extreme that they name: `east_west_harmonic`: Distinct; positions 2 j and 2 j + 1 hold m and 1279 - m for some m below 640; 0 is among them. `patch_active_entries`: the live slots of a tile come first; the last tile is full. For a slot of tile t, sea_southern_parallel and sea_southern_parallel + 1 lie in t * 80 - 8 to (t + 1) * 80 + 7; they do not decrease along a tile's live slots. `air_paired_cells`: for a latitude of band t both taps are live slots of tiles t - 1, t or t + 1, the first one of tile t, and the two differ.
All inputs are finite; a program needn't handle non-finite values.
Results may differ from a plain program's by a relative error of at most 0.014.
Values may be sent and summed in bfloat16 or wider, within the bound.
A program may use at most 64 MiB of HBM per device.

v0:
```python
import math

import jax
import jax.numpy as jnp
from jax import lax
from jax.sharding import PartitionSpec as P

PARALLEL_NUMBER = 1280
MARG = 8


degree_damping = 2e-06
ocean_step = 0.5
mixing_diagonal = 0.95
synth_divisor = 4.0


def with_halo(shard, sides, width):
    for axis, dim in sides:
        size, length = (lax.axis_size(axis), shard.shape[dim])
        up = [(i, (i + 1) % size) for i in range(size - 1)]
        down = [(j, i) for i, j in up]
        last = lax.slice_in_dim(shard, length - width, length, axis=dim)
        first = lax.slice_in_dim(shard, 0, width, axis=dim)
        before = lax.ppermute(last, axis, up)
        after = lax.ppermute(first, axis, down)
        shard = jnp.concatenate([before, shard, after], axis=dim)
    return shard


def damping_table(wave_values, degree_count):
    degrees = wave_values[:, None] + jnp.arange(degree_count, dtype=jnp.int32)[None, :]
    degree_float = degrees.astype(jnp.float32)
    factor = 1.0 / (1.0 + degree_damping * degree_float * (degree_float + 1.0))
    return jnp.where(degrees < degree_count, factor, jnp.zeros_like(factor))


def zonal_table(wave_values, lon_count):
    longitude = jnp.arange(lon_count, dtype=jnp.int32)
    phases = wave_values[:, None] * longitude[None, :] % lon_count
    angles = phases.astype(jnp.float32) * (2.0 * math.pi / lon_count)
    stacked = jnp.stack([jnp.cos(angles), -jnp.sin(angles)], axis=1)
    return stacked.reshape(2 * wave_values.shape[0], lon_count).astype(jnp.bfloat16)


def padded_transform(values, tables, damping):
    row_count = values.shape[0]
    lat_count = values.shape[1]
    wave_count = tables.shape[0]
    shaped = values.reshape(row_count, lat_count, wave_count, 2)
    spectral = jnp.einsum("rlmc,mln->rmnc", shaped, tables, preferred_element_type=jnp.float32)
    damped = (spectral * damping[None, :, :, None]).astype(jnp.bfloat16)
    synthesis = jnp.einsum("rmnc,mln->rlmc", damped, tables, preferred_element_type=jnp.float32)
    synthesis = synthesis * (1.0 / (synth_divisor * math.sqrt(tables.shape[2])))
    return synthesis.astype(jnp.bfloat16).reshape(row_count, lat_count, wave_count * 2)


def per_device(
    air_fourier_coefficients,
    quadrature_factor,
    associated_polynomial_table,
    east_west_harmonic,
    boundary_diffusion,
    bulk_transfer_coefficient,
    skin_heat_earlier,
    sea_boundary_values,
    sea_damping_speed,
    sea_coupling_matrix,
    patch_active_entries,
    sea_southern_parallel,
    sea_northern_share,
    air_paired_cells,
    air_second_share,
):
    band_index = lax.axis_index("band")
    lev_index = lax.axis_index("lev")
    field_local = air_fourier_coefficients.shape[0]
    height_pile = air_fourier_coefficients.shape[1]
    lat_local = air_fourier_coefficients.shape[2]
    column_count = air_fourier_coefficients.shape[3]
    row_count = field_local * height_pile
    owned = associated_polynomial_table.shape[0]
    degree_count = associated_polynomial_table.shape[2]
    wave_values = lax.dynamic_slice_in_dim(east_west_harmonic, band_index * owned, owned, 0)
    damping = damping_table(wave_values, degree_count)

    def transform(values):
        return padded_transform(values, associated_polynomial_table, damping)

    identity_block = jnp.eye(height_pile, dtype=jnp.float32)[None, :, :, None]
    mixing = (
        mixing_diagonal * identity_block
        + boundary_diffusion
        - jnp.transpose(boundary_diffusion, (0, 2, 1, 3))
    )
    weight = quadrature_factor * (1.0 / math.sqrt(PARALLEL_NUMBER))

    def march_air_model(air_model_present, skin_heat_present):
        scaled = (air_model_present * weight[None, None, :, None]).astype(jnp.bfloat16)
        scaled = scaled.reshape(row_count, lat_local, column_count)
        by_wave = lax.all_to_all(scaled, "band", split_axis=2, concat_axis=1, tiled=True)
        synthesis = transform(by_wave)
        returned = lax.all_to_all(synthesis, "band", split_axis=1, concat_axis=2, tiled=True)
        synthesis_field = returned.reshape(
            field_local, height_pile, lat_local, column_count
        ).astype(jnp.float32)
        halfway_point = air_model_present - synthesis_field
        bottom_sheet = bulk_transfer_coefficient[:, :, None] * (
            skin_heat_present - halfway_point[:, height_pile - 1]
        )
        mixed_state = jnp.einsum(
            "flpa,fpac->flac", mixing, halfway_point, precision=lax.Precision.HIGHEST
        )
        mixed_state = mixed_state.at[:, height_pile - 1].add(bottom_sheet)
        return (mixed_state, bottom_sheet.astype(jnp.bfloat16))

    air_coefficients_end, forcing_series = lax.scan(
        march_air_model, air_fourier_coefficients, skin_heat_earlier
    )
    slot_rows = sea_boundary_values.shape[1]
    extended = with_halo(forcing_series, (("band", 2),), MARG)
    rim_rows = lat_local + 2 * MARG
    lowest = band_index * lat_local - MARG
    live_slot = jnp.arange(slot_rows, dtype=jnp.int32) < patch_active_entries[0]
    offsets = (sea_southern_parallel - lowest)[:, None]
    rim_index = jnp.arange(rim_rows, dtype=jnp.int32)[None, :]
    low_weight = jnp.where(live_slot, 1.0 - sea_northern_share, jnp.zeros_like(sea_northern_share))[
        :, None
    ]
    high_weight = jnp.where(live_slot, sea_northern_share, jnp.zeros_like(sea_northern_share))[
        :, None
    ]
    flux_taps = jnp.where(rim_index == offsets, low_weight, 0.0) + jnp.where(
        rim_index == offsets + 1, high_weight, 0.0
    )
    flux_taps = flux_taps.astype(jnp.bfloat16)
    ocean_flux = jnp.einsum(
        "sa,kfac->kfsc", flux_taps, extended, preferred_element_type=jnp.float32
    ).astype(jnp.bfloat16)
    lon_count = sea_boundary_values.shape[2]
    zonal_basis = zonal_table(east_west_harmonic, lon_count)
    synth_scale = 1.0 / math.sqrt(zonal_basis.shape[0])
    skew_full = sea_coupling_matrix - sea_coupling_matrix.T
    skew_mine = lax.dynamic_slice_in_dim(skew_full, lev_index * field_local, field_local, 0)

    def ocean_advance(ocean_now, flux_now):
        forcing = (
            jnp.einsum("fsc,cx->fsx", flux_now, zonal_basis, preferred_element_type=jnp.float32)
            * synth_scale
        )
        gathered = lax.all_gather(ocean_now.astype(jnp.bfloat16), "lev", axis=0, tiled=True)
        coupled = jnp.zeros_like(ocean_now)
        for field_index in range(gathered.shape[0]):
            coupled = (
                coupled
                + skew_mine[:, field_index][:, None, None]
                * gathered[field_index].astype(jnp.float32)[None]
            )
        updated = (ocean_now + ocean_step * (coupled - forcing)) / (
            1.0 + ocean_step * sea_damping_speed
        )
        return (updated, updated.astype(jnp.bfloat16))

    sea_values_end, ocean_wave = lax.scan(ocean_advance, sea_boundary_values, ocean_flux)
    ocean_coef = jnp.einsum(
        "kfsx,cx->kfsc", ocean_wave, zonal_basis, preferred_element_type=jnp.float32
    )
    ocean_coef = (ocean_coef * (1.0 / math.sqrt(lon_count))).astype(jnp.bfloat16)
    neighbours = with_halo(ocean_coef, (("band", 2),), slot_rows)
    base_slot = (band_index - 1) * slot_rows
    slot_index = jnp.arange(3 * slot_rows, dtype=jnp.int32)[None, :]
    first_local = (air_paired_cells[0] - base_slot)[:, None]
    second_local = (air_paired_cells[1] - base_slot)[:, None]
    return_taps = jnp.where(
        slot_index == first_local, (1.0 - air_second_share)[:, None], 0.0
    ) + jnp.where(slot_index == second_local, air_second_share[:, None], 0.0)
    return_taps = return_taps.astype(jnp.bfloat16)
    skin_heat_newest = jnp.einsum(
        "ga,kfac->kfgc", return_taps, neighbours, preferred_element_type=jnp.float32
    )
    return (air_coefficients_end, sea_values_end, skin_heat_newest)


def solution(mesh):
    return jax.shard_map(
        per_device,
        mesh=mesh,
        in_specs=(
            P("lev", None, "band", None),
            P("band"),
            P("band", None, None),
            P(),
            P("lev", None, None, "band"),
            P("lev", "band"),
            P(None, "lev", "band", None),
            P("lev", "band", None),
            P("lev", "band", None),
            P(),
            P("band"),
            P("band"),
            P("band"),
            P(None, "band"),
            P("band"),
        ),
        out_specs=(
            P("lev", None, "band", None),
            P("lev", "band", None),
            P(None, "lev", "band", None),
        ),
        check_vma=False,
    )
```

profile of v0, /device:TPU:11, one launch (start us, length us, event | category | flops | bytes accessed | tf_op | source)
XLA Modules:
  0.0 1302.1 jit_solution(8475051857422284199)
XLA Ops:
  8.3 1166.4 %while.29 = (s32[]{:T(128)}, f32[2,16,80,128]{3,1,2,0:T(8,128)S(1)}, bf16[12,2,80,128]{3,2,1,0:T(8,128)(2,1)}, f32[80]{0:T(128)S(1)}, bf16[4,1280,1280]{2,1,0:T(...) while((s32[]{:T(128)}, ...), condition=%wide.region_1.2_spmd.clone, body=%wide.region_0.1_spmd.clone.sunk | while | flops 1743098880 | bytes 56248172 | solution.py:117
  17.1 24.8 %all-to-all-done = bf16[32,80,128]{1,0,2:T(8,128)(2,1)S(1)} async-done(((bf16[32,80,128]{1,0,2:T(8,128)(2,1)}), bf16[32,80,128]{1,0,2:T(8,128)(2,1)S(1)}, u32[]{:S(2)}, u32[]{:S(2)}) %all-to-all-start) | async-done | bytes 655392 | tf_op jit(solution)/shard_map/while/body/eval_jaxpr/all_to_all | solution.py:101
  69.4 16.4 %all-to-all-done.1 = bf16[16,2,10240]{2,1,0:T(2,128)(2,1)S(1)} async-done(((bf16[16,2,10240]{2,1,0:T(2,128)(2,1)}), bf16[16,2,10240]{2,1,0:T(2,128)(2,1)S(1)}, u32[]{:S(2)}, u32[]{:S(2)}) %all-to-all-start.1) | async-done | bytes 655392 | tf_op jit(solution)/shard_map/while/body/eval_jaxpr/all_to_all | solution.py:103
  114.1 24.8 %all-to-all-done = bf16[32,80,128]{1,0,2:T(8,128)(2,1)S(1)} async-done(((bf16[32,80,128]{1,0,2:T(8,128)(2,1)}), bf16[32,80,128]{1,0,2:T(8,128)(2,1)S(1)}, u32[]{:S(2)}, u32[]{:S(2)}) %all-to-all-start) | async-done | bytes 655392 | tf_op jit(solution)/shard_map/while/body/eval_jaxpr/all_to_all | solution.py:101
  166.4 16.4 %all-to-all-done.1 = bf16[16,2,10240]{2,1,0:T(2,128)(2,1)S(1)} async-done(((bf16[16,2,10240]{2,1,0:T(2,128)(2,1)}), bf16[16,2,10240]{2,1,0:T(2,128)(2,1)S(1)}, u32[]{:S(2)}, u32[]{:S(2)}) %all-to-all-start.1) | async-done | bytes 655392 | tf_op jit(solution)/shard_map/while/body/eval_jaxpr/all_to_all | solution.py:103
  211.2 24.8 %all-to-all-done = bf16[32,80,128]{1,0,2:T(8,128)(2,1)S(1)} async-done(((bf16[32,80,128]{1,0,2:T(8,128)(2,1)}), bf16[32,80,128]{1,0,2:T(8,128)(2,1)S(1)}, u32[]{:S(2)}, u32[]{:S(2)}) %all-to-all-start) | async-done | bytes 655392 | tf_op jit(solution)/shard_map/while/body/eval_jaxpr/all_to_all | solution.py:101
  263.5 16.4 %all-to-all-done.1 = bf16[16,2,10240]{2,1,0:T(2,128)(2,1)S(1)} async-done(((bf16[16,2,10240]{2,1,0:T(2,128)(2,1)}), bf16[16,2,10240]{2,1,0:T(2,128)(2,1)S(1)}, u32[]{:S(2)}, u32[]{:S(2)}) %all-to-all-start.1) | async-done | bytes 655392 | tf_op jit(solution)/shard_map/while/body/eval_jaxpr/all_to_all | solution.py:103
  308.2 24.8 %all-to-all-done = bf16[32,80,128]{1,0,2:T(8,128)(2,1)S(1)} async-done(((bf16[32,80,128]{1,0,2:T(8,128)(2,1)}), bf16[32,80,128]{1,0,2:T(8,128)(2,1)S(1)}, u32[]{:S(2)}, u32[]{:S(2)}) %all-to-all-start) | async-done | bytes 655392 | tf_op jit(solution)/shard_map/while/body/eval_jaxpr/all_to_all | solution.py:101
  360.5 16.4 %all-to-all-done.1 = bf16[16,2,10240]{2,1,0:T(2,128)(2,1)S(1)} async-done(((bf16[16,2,10240]{2,1,0:T(2,128)(2,1)}), bf16[16,2,10240]{2,1,0:T(2,128)(2,1)S(1)}, u32[]{:S(2)}, u32[]{:S(2)}) %all-to-all-start.1) | async-done | bytes 655392 | tf_op jit(solution)/shard_map/while/body/eval_jaxpr/all_to_all | solution.py:103
  405.3 24.8 %all-to-all-done = bf16[32,80,128]{1,0,2:T(8,128)(2,1)S(1)} async-done(((bf16[32,80,128]{1,0,2:T(8,128)(2,1)}), bf16[32,80,128]{1,0,2:T(8,128)(2,1)S(1)}, u32[]{:S(2)}, u32[]{:S(2)}) %all-to-all-start) | async-done | bytes 655392 | tf_op jit(solution)/shard_map/while/body/eval_jaxpr/all_to_all | solution.py:101
  457.6 16.4 %all-to-all-done.1 = bf16[16,2,10240]{2,1,0:T(2,128)(2,1)S(1)} async-done(((bf16[16,2,10240]{2,1,0:T(2,128)(2,1)}), bf16[16,2,10240]{2,1,0:T(2,128)(2,1)S(1)}, u32[]{:S(2)}, u32[]{:S(2)}) %all-to-all-start.1) | async-done | bytes 655392 | tf_op jit(solution)/shard_map/while/body/eval_jaxpr/all_to_all | solution.py:103
  502.4 24.8 %all-to-all-done = bf16[32,80,128]{1,0,2:T(8,128)(2,1)S(1)} async-done(((bf16[32,80,128]{1,0,2:T(8,128)(2,1)}), bf16[32,80,128]{1,0,2:T(8,128)(2,1)S(1)}, u32[]{:S(2)}, u32[]{:S(2)}) %all-to-all-start) | async-done | bytes 655392 | tf_op jit(solution)/shard_map/while/body/eval_jaxpr/all_to_all | solution.py:101
  554.6 16.4 %all-to-all-done.1 = bf16[16,2,10240]{2,1,0:T(2,128)(2,1)S(1)} async-done(((bf16[16,2,10240]{2,1,0:T(2,128)(2,1)}), bf16[16,2,10240]{2,1,0:T(2,128)(2,1)S(1)}, u32[]{:S(2)}, u32[]{:S(2)}) %all-to-all-start.1) | async-done | bytes 655392 | tf_op jit(solution)/shard_map/while/body/eval_jaxpr/all_to_all | solution.py:103
  599.4 24.8 %all-to-all-done = bf16[32,80,128]{1,0,2:T(8,128)(2,1)S(1)} async-done(((bf16[32,80,128]{1,0,2:T(8,128)(2,1)}), bf16[32,80,128]{1,0,2:T(8,128)(2,1)S(1)}, u32[]{:S(2)}, u32[]{:S(2)}) %all-to-all-start) | async-done | bytes 655392 | tf_op jit(solution)/shard_map/while/body/eval_jaxpr/all_to_all | solution.py:101
  651.7 16.4 %all-to-all-done.1 = bf16[16,2,10240]{2,1,0:T(2,128)(2,1)S(1)} async-done(((bf16[16,2,10240]{2,1,0:T(2,128)(2,1)}), bf16[16,2,10240]{2,1,0:T(2,128)(2,1)S(1)}, u32[]{:S(2)}, u32[]{:S(2)}) %all-to-all-start.1) | async-done | bytes 655392 | tf_op jit(solution)/shard_map/while/body/eval_jaxpr/all_to_all | solution.py:103
  696.5 24.8 %all-to-all-done = bf16[32,80,128]{1,0,2:T(8,128)(2,1)S(1)} async-done(((bf16[32,80,128]{1,0,2:T(8,128)(2,1)}), bf16[32,80,128]{1,0,2:T(8,128)(2,1)S(1)}, u32[]{:S(2)}, u32[]{:S(2)}) %all-to-all-start) | async-done | bytes 655392 | tf_op jit(solution)/shard_map/while/body/eval_jaxpr/all_to_all | solution.py:101
  748.8 16.4 %all-to-all-done.1 = bf16[16,2,10240]{2,1,0:T(2,128)(2,1)S(1)} async-done(((bf16[16,2,10240]{2,1,0:T(2,128)(2,1)}), bf16[16,2,10240]{2,1,0:T(2,128)(2,1)S(1)}, u32[]{:S(2)}, u32[]{:S(2)}) %all-to-all-start.1) | async-done | bytes 655392 | tf_op jit(solution)/shard_map/while/body/eval_jaxpr/all_to_all | solution.py:103
  793.5 24.8 %all-to-all-done = bf16[32,80,128]{1,0,2:T(8,128)(2,1)S(1)} async-done(((bf16[32,80,128]{1,0,2:T(8,128)(2,1)}), bf16[32,80,128]{1,0,2:T(8,128)(2,1)S(1)}, u32[]{:S(2)}, u32[]{:S(2)}) %all-to-all-start) | async-done | bytes 655392 | tf_op jit(solution)/shard_map/while/body/eval_jaxpr/all_to_all | solution.py:101
  845.8 16.4 %all-to-all-done.1 = bf16[16,2,10240]{2,1,0:T(2,128)(2,1)S(1)} async-done(((bf16[16,2,10240]{2,1,0:T(2,128)(2,1)}), bf16[16,2,10240]{2,1,0:T(2,128)(2,1)S(1)}, u32[]{:S(2)}, u32[]{:S(2)}) %all-to-all-start.1) | async-done | bytes 655392 | tf_op jit(solution)/shard_map/while/body/eval_jaxpr/all_to_all | solution.py:103
  890.6 24.8 %all-to-all-done = bf16[32,80,128]{1,0,2:T(8,128)(2,1)S(1)} async-done(((bf16[32,80,128]{1,0,2:T(8,128)(2,1)}), bf16[32,80,128]{1,0,2:T(8,128)(2,1)S(1)}, u32[]{:S(2)}, u32[]{:S(2)}) %all-to-all-start) | async-done | bytes 655392 | tf_op jit(solution)/shard_map/while/body/eval_jaxpr/all_to_all | solution.py:101
  987.6 24.8 %all-to-all-done = bf16[32,80,128]{1,0,2:T(8,128)(2,1)S(1)} async-done(((bf16[32,80,128]{1,0,2:T(8,128)(2,1)}), bf16[32,80,128]{1,0,2:T(8,128)(2,1)S(1)}, u32[]{:S(2)}, u32[]{:S(2)}) %all-to-all-start) | async-done | bytes 655392 | tf_op jit(solution)/shard_map/while/body/eval_jaxpr/all_to_all | solution.py:101
  1084.7 24.8 %all-to-all-done = bf16[32,80,128]{1,0,2:T(8,128)(2,1)S(1)} async-done(((bf16[32,80,128]{1,0,2:T(8,128)(2,1)}), bf16[32,80,128]{1,0,2:T(8,128)(2,1)S(1)}, u32[]{:S(2)}, u32[]{:S(2)}) %all-to-all-start) | async-done | bytes 655392 | tf_op jit(solution)/shard_map/while/body/eval_jaxpr/all_to_all | solution.py:101
  1187.4 85.0 %while.28 = (s32[]{:T(128)}, f32[2,32,1440]{2,1,0:T(8,128)S(1)}, bf16[12,2,32,1440]{3,2,1,0:T(8,128)(2,1)}, f32[2,4]{0,1:T(4,128)S(1)}, bf16[12,2,32,128]{3,2,1,...) while((s32[]{:T(128)}, f32[2,32,1440]{2,1,0:T(8,128)S(1)}, ...), condition=%wide.region_3.4_spmd, body=%wide.region_2.3_spmd.sunk | while | flops 25251840 | bytes 4738197 | solution.py:164
  1275.0 17.9 %collective-permute-start.2 = (bf16[12,2,32,128]{3,2,1,0:T(8,128)(2,1)S(1)}, bf16[12,2,32,128]{3,2,1,0:T(8,128)(2,1)S(1)}, u32[]{:S(2)}, u32[]{:S(2)}) collective-permute-start(bf16[12,2,32,128]{3,2,1,0:T(8,128)(2,1)S(1)} %fusion.45), channel_id=1, source_target_pairs={{0,2},{2,4},{4,6},{6,8},{8,10},{10,12},{12,14},{14,16},{16,18},{18... | collective-permute-start | bytes 589832 | tf_op jit(solution)/shard_map/ppermute | solution.py:25
  (446 shorter events, 835.2 us)
Async XLA Ops:
  10.4 31.4 %all-to-all-start = ((bf16[32,80,128]{1,0,2:T(8,128)(2,1)}), bf16[32,80,128]{1,0,2:T(8,128)(2,1)S(1)}, u32[]{:S(2)}, u32[]{:S(2)}) async-start(bf16[32,80,128]{1,0,2:T(8,128)(2,1)} %copy.135), calls=%async_computation | async-start | bytes 2097152 | tf_op jit(solution)/shard_map/while/body/eval_jaxpr/all_to_all | solution.py:101
  64.4 21.4 %all-to-all-start.1 = ((bf16[16,2,10240]{2,1,0:T(2,128)(2,1)}), bf16[16,2,10240]{2,1,0:T(2,128)(2,1)S(1)}, u32[]{:S(2)}, u32[]{:S(2)}) async-start(bf16[16,2,10240]{2,1,0:T(2,128)(2,1)} %reshape.235), calls=%async_computation.1 | async-start | bytes 1310720 | tf_op jit(solution)/shard_map/while/body/eval_jaxpr/all_to_all | solution.py:103
  109.1 29.8 %all-to-all-start = ((bf16[32,80,128]{1,0,2:T(8,128)(2,1)}), bf16[32,80,128]{1,0,2:T(8,128)(2,1)S(1)}, u32[]{:S(2)}, u32[]{:S(2)}) async-start(bf16[32,80,128]{1,0,2:T(8,128)(2,1)} %copy.135), calls=%async_computation | async-start | bytes 2097152 | tf_op jit(solution)/shard_map/while/body/eval_jaxpr/all_to_all | solution.py:101
  161.5 21.4 %all-to-all-start.1 = ((bf16[16,2,10240]{2,1,0:T(2,128)(2,1)}), bf16[16,2,10240]{2,1,0:T(2,128)(2,1)S(1)}, u32[]{:S(2)}, u32[]{:S(2)}) async-start(bf16[16,2,10240]{2,1,0:T(2,128)(2,1)} %reshape.235), calls=%async_computation.1 | async-start | bytes 1310720 | tf_op jit(solution)/shard_map/while/body/eval_jaxpr/all_to_all | solution.py:103
  206.2 29.8 %all-to-all-start = ((bf16[32,80,128]{1,0,2:T(8,128)(2,1)}), bf16[32,80,128]{1,0,2:T(8,128)(2,1)S(1)}, u32[]{:S(2)}, u32[]{:S(2)}) async-start(bf16[32,80,128]{1,0,2:T(8,128)(2,1)} %copy.135), calls=%async_computation | async-start | bytes 2097152 | tf_op jit(solution)/shard_map/while/body/eval_jaxpr/all_to_all | solution.py:101
  258.5 21.4 %all-to-all-start.1 = ((bf16[16,2,10240]{2,1,0:T(2,128)(2,1)}), bf16[16,2,10240]{2,1,0:T(2,128)(2,1)S(1)}, u32[]{:S(2)}, u32[]{:S(2)}) async-start(bf16[16,2,10240]{2,1,0:T(2,128)(2,1)} %reshape.235), calls=%async_computation.1 | async-start | bytes 1310720 | tf_op jit(solution)/shard_map/while/body/eval_jaxpr/all_to_all | solution.py:103
  303.2 29.8 %all-to-all-start = ((bf16[32,80,128]{1,0,2:T(8,128)(2,1)}), bf16[32,80,128]{1,0,2:T(8,128)(2,1)S(1)}, u32[]{:S(2)}, u32[]{:S(2)}) async-start(bf16[32,80,128]{1,0,2:T(8,128)(2,1)} %copy.135), calls=%async_computation | async-start | bytes 2097152 | tf_op jit(solution)/shard_map/while/body/eval_jaxpr/all_to_all | solution.py:101
  355.6 21.4 %all-to-all-start.1 = ((bf16[16,2,10240]{2,1,0:T(2,128)(2,1)}), bf16[16,2,10240]{2,1,0:T(2,128)(2,1)S(1)}, u32[]{:S(2)}, u32[]{:S(2)}) async-start(bf16[16,2,10240]{2,1,0:T(2,128)(2,1)} %reshape.235), calls=%async_computation.1 | async-start | bytes 1310720 | tf_op jit(solution)/shard_map/while/body/eval_jaxpr/all_to_all | solution.py:103
  400.3 29.8 %all-to-all-start = ((bf16[32,80,128]{1,0,2:T(8,128)(2,1)}), bf16[32,80,128]{1,0,2:T(8,128)(2,1)S(1)}, u32[]{:S(2)}, u32[]{:S(2)}) async-start(bf16[32,80,128]{1,0,2:T(8,128)(2,1)} %copy.135), calls=%async_computation | async-start | bytes 2097152 | tf_op jit(solution)/shard_map/while/body/eval_jaxpr/all_to_all | solution.py:101
  452.7 21.4 %all-to-all-start.1 = ((bf16[16,2,10240]{2,1,0:T(2,128)(2,1)}), bf16[16,2,10240]{2,1,0:T(2,128)(2,1)S(1)}, u32[]{:S(2)}, u32[]{:S(2)}) async-start(bf16[16,2,10240]{2,1,0:T(2,128)(2,1)} %reshape.235), calls=%async_computation.1 | async-start | bytes 1310720 | tf_op jit(solution)/shard_map/while/body/eval_jaxpr/all_to_all | solution.py:103
  497.3 29.8 %all-to-all-start = ((bf16[32,80,128]{1,0,2:T(8,128)(2,1)}), bf16[32,80,128]{1,0,2:T(8,128)(2,1)S(1)}, u32[]{:S(2)}, u32[]{:S(2)}) async-start(bf16[32,80,128]{1,0,2:T(8,128)(2,1)} %copy.135), calls=%async_computation | async-start | bytes 2097152 | tf_op jit(solution)/shard_map/while/body/eval_jaxpr/all_to_all | solution.py:101
  549.7 21.4 %all-to-all-start.1 = ((bf16[16,2,10240]{2,1,0:T(2,128)(2,1)}), bf16[16,2,10240]{2,1,0:T(2,128)(2,1)S(1)}, u32[]{:S(2)}, u32[]{:S(2)}) async-start(bf16[16,2,10240]{2,1,0:T(2,128)(2,1)} %reshape.235), calls=%async_computation.1 | async-start | bytes 1310720 | tf_op jit(solution)/shard_map/while/body/eval_jaxpr/all_to_all | solution.py:103
  594.4 29.8 %all-to-all-start = ((bf16[32,80,128]{1,0,2:T(8,128)(2,1)}), bf16[32,80,128]{1,0,2:T(8,128)(2,1)S(1)}, u32[]{:S(2)}, u32[]{:S(2)}) async-start(bf16[32,80,128]{1,0,2:T(8,128)(2,1)} %copy.135), calls=%async_computation | async-start | bytes 2097152 | tf_op jit(solution)/shard_map/while/body/eval_jaxpr/all_to_all | solution.py:101
  646.8 21.4 %all-to-all-start.1 = ((bf16[16,2,10240]{2,1,0:T(2,128)(2,1)}), bf16[16,2,10240]{2,1,0:T(2,128)(2,1)S(1)}, u32[]{:S(2)}, u32[]{:S(2)}) async-start(bf16[16,2,10240]{2,1,0:T(2,128)(2,1)} %reshape.235), calls=%async_computation.1 | async-start | bytes 1310720 | tf_op jit(solution)/shard_map/while/body/eval_jaxpr/all_to_all | solution.py:103
  691.4 29.8 %all-to-all-start = ((bf16[32,80,128]{1,0,2:T(8,128)(2,1)}), bf16[32,80,128]{1,0,2:T(8,128)(2,1)S(1)}, u32[]{:S(2)}, u32[]{:S(2)}) async-start(bf16[32,80,128]{1,0,2:T(8,128)(2,1)} %copy.135), calls=%async_computation | async-start | bytes 2097152 | tf_op jit(solution)/shard_map/while/body/eval_jaxpr/all_to_all | solution.py:101
  743.8 21.4 %all-to-all-start.1 = ((bf16[16,2,10240]{2,1,0:T(2,128)(2,1)}), bf16[16,2,10240]{2,1,0:T(2,128)(2,1)S(1)}, u32[]{:S(2)}, u32[]{:S(2)}) async-start(bf16[16,2,10240]{2,1,0:T(2,128)(2,1)} %reshape.235), calls=%async_computation.1 | async-start | bytes 1310720 | tf_op jit(solution)/shard_map/while/body/eval_jaxpr/all_to_all | solution.py:103
  788.5 29.8 %all-to-all-start = ((bf16[32,80,128]{1,0,2:T(8,128)(2,1)}), bf16[32,80,128]{1,0,2:T(8,128)(2,1)S(1)}, u32[]{:S(2)}, u32[]{:S(2)}) async-start(bf16[32,80,128]{1,0,2:T(8,128)(2,1)} %copy.135), calls=%async_computation | async-start | bytes 2097152 | tf_op jit(solution)/shard_map/while/body/eval_jaxpr/all_to_all | solution.py:101
  840.9 21.4 %all-to-all-start.1 = ((bf16[16,2,10240]{2,1,0:T(2,128)(2,1)}), bf16[16,2,10240]{2,1,0:T(2,128)(2,1)S(1)}, u32[]{:S(2)}, u32[]{:S(2)}) async-start(bf16[16,2,10240]{2,1,0:T(2,128)(2,1)} %reshape.235), calls=%async_computation.1 | async-start | bytes 1310720 | tf_op jit(solution)/shard_map/while/body/eval_jaxpr/all_to_all | solution.py:103
  885.5 29.8 %all-to-all-start = ((bf16[32,80,128]{1,0,2:T(8,128)(2,1)}), bf16[32,80,128]{1,0,2:T(8,128)(2,1)S(1)}, u32[]{:S(2)}, u32[]{:S(2)}) async-start(bf16[32,80,128]{1,0,2:T(8,128)(2,1)} %copy.135), calls=%async_computation | async-start | bytes 2097152 | tf_op jit(solution)/shard_map/while/body/eval_jaxpr/all_to_all | solution.py:101
  937.9 21.4 %all-to-all-start.1 = ((bf16[16,2,10240]{2,1,0:T(2,128)(2,1)}), bf16[16,2,10240]{2,1,0:T(2,128)(2,1)S(1)}, u32[]{:S(2)}, u32[]{:S(2)}) async-start(bf16[16,2,10240]{2,1,0:T(2,128)(2,1)} %reshape.235), calls=%async_computation.1 | async-start | bytes 1310720 | tf_op jit(solution)/shard_map/while/body/eval_jaxpr/all_to_all | solution.py:103
  982.6 29.8 %all-to-all-start = ((bf16[32,80,128]{1,0,2:T(8,128)(2,1)}), bf16[32,80,128]{1,0,2:T(8,128)(2,1)S(1)}, u32[]{:S(2)}, u32[]{:S(2)}) async-start(bf16[32,80,128]{1,0,2:T(8,128)(2,1)} %copy.135), calls=%async_computation | async-start | bytes 2097152 | tf_op jit(solution)/shard_map/while/body/eval_jaxpr/all_to_all | solution.py:101
  1035.0 21.4 %all-to-all-start.1 = ((bf16[16,2,10240]{2,1,0:T(2,128)(2,1)}), bf16[16,2,10240]{2,1,0:T(2,128)(2,1)S(1)}, u32[]{:S(2)}, u32[]{:S(2)}) async-start(bf16[16,2,10240]{2,1,0:T(2,128)(2,1)} %reshape.235), calls=%async_computation.1 | async-start | bytes 1310720 | tf_op jit(solution)/shard_map/while/body/eval_jaxpr/all_to_all | solution.py:103
  1079.6 29.8 %all-to-all-start = ((bf16[32,80,128]{1,0,2:T(8,128)(2,1)}), bf16[32,80,128]{1,0,2:T(8,128)(2,1)S(1)}, u32[]{:S(2)}, u32[]{:S(2)}) async-start(bf16[32,80,128]{1,0,2:T(8,128)(2,1)} %copy.135), calls=%async_computation | async-start | bytes 2097152 | tf_op jit(solution)/shard_map/while/body/eval_jaxpr/all_to_all | solution.py:101
  1132.0 21.4 %all-to-all-start.1 = ((bf16[16,2,10240]{2,1,0:T(2,128)(2,1)}), bf16[16,2,10240]{2,1,0:T(2,128)(2,1)S(1)}, u32[]{:S(2)}, u32[]{:S(2)}) async-start(bf16[16,2,10240]{2,1,0:T(2,128)(2,1)} %reshape.235), calls=%async_computation.1 | async-start | bytes 1310720 | tf_op jit(solution)/shard_map/while/body/eval_jaxpr/all_to_all | solution.py:103
  (53 other events, 3683.8 us)
where the time goes:
time: 1310 us; the launch traced here: 1300 us
  waiting for transfers between devices  501 us (38%)
  local copies, waits for them, and re-layouts  316 us (24%)
  matrix products  218 us (17%)
  starting transfers between devices  146 us (11%)
  blocking collectives  69.7 us (5%)
  other arithmetic  48.1 us (4%)
    all_to_all x12, waiting for transfers between devices, march_air_model(): lax.all_to_all(scaled, 'band', split_axis=2, concat_axis=1, tiled=True)  297 us
    all_to_all x12, waiting for transfers between devices, march_air_model(): lax.all_to_all(synthesis, 'band', split_axis=1, concat_axis=2, tiled=True)  197 us
    dot_general x12, matrix products, padded_transform(): jnp.einsum('rmnc,mln->rlmc', damped, tables, preferred_element_type=jnp.f...  176 us
    all_gather x12, blocking collectives, ocean_advance(): lax.all_gather(ocean_now.astype(jnp.bfloat16), 'lev', axis=0, tiled=True)  69.7 us
    convert_element_type x36, local copies, waits for them, and re-layouts, march_air_model(): synthesis_field = returned.reshape(field_local, height_pile, lat_local, c...  68.3 us
    while x96, local copies, waits for them, and re-layouts  63.5 us
    all_to_all x12, starting transfers between devices, march_air_model(): lax.all_to_all(scaled, 'band', split_axis=2, concat_axis=1, tiled=True)  61 us
    all_to_all x12, starting transfers between devices, march_air_model(): lax.all_to_all(synthesis, 'band', split_axis=1, concat_axis=2, tiled=True)  59.2 us
  transfers between devices with their start and end apart: 28, of which 26 were waited for; matrix products, arithmetic and copies ran while one was open for 0% of the time, Pallas kernels for 0%

commit v1 on v0

v1 whole, which is shorter than its diff:
```python
import functools
import math

import jax
import jax.numpy as jnp
from jax import lax
from jax.experimental import pallas as pl
from jax.experimental.pallas import tpu as pltpu
from jax.sharding import PartitionSpec as P

degree_damping = 2e-06
ocean_step = 0.5
mixing_diagonal = 0.95
synth_divisor = 4.0

LANES = 128
WIDE = 256
SUBLANES = 8
VMEM_LIMIT = 52 * 1024 * 1024


def zonal_table(wave_values, lon_count):
    longitude = jnp.arange(lon_count, dtype=jnp.int32)
    phases = wave_values[:, None] * longitude[None, :] % lon_count
    angles = phases.astype(jnp.float32) * (2.0 * math.pi / lon_count)
    stacked = jnp.stack([jnp.cos(angles), -jnp.sin(angles)], axis=1)
    return stacked.reshape(2 * wave_values.shape[0], lon_count).astype(jnp.bfloat16)


def live_tiles(wave_values, degree_count, tile_count):
    live = degree_count - wave_values
    blocks = (live + LANES - 1) // LANES
    ends = jnp.cumsum(blocks)
    tile = jnp.arange(tile_count, dtype=jnp.int32)
    wave = jnp.sum((tile[:, None] >= ends[None, :]).astype(jnp.int32), axis=1)
    wave = jnp.minimum(wave, wave_values.shape[0] - 1)
    one_hot = wave[:, None] == jnp.arange(wave_values.shape[0], dtype=jnp.int32)[None, :]
    start = jnp.sum(jnp.where(one_hot, (ends - blocks)[None, :], 0), axis=1)
    block = jnp.minimum(tile - start, degree_count // LANES - 1)
    owner = jnp.sum(jnp.where(one_hot, wave_values[None, :], 0), axis=1)
    degree = (owner + block * LANES)[:, None] + jnp.arange(LANES, dtype=jnp.int32)[None, :]
    used = (tile < ends[-1])[:, None] & (degree < degree_count)
    degree_float = degree.astype(jnp.float32)
    factor = 1.0 / (1.0 + degree_damping * degree_float * (degree_float + 1.0))
    factor = jnp.where(used, factor, 0.0).reshape(tile_count * LANES)
    column_wave = jnp.repeat(jnp.arange(wave_values.shape[0], dtype=jnp.int32), 2)
    owner_wave = jnp.repeat(wave, LANES)
    damping = jnp.where(column_wave[:, None] == owner_wave[None, :], factor[None, :], 0.0)
    return wave.astype(jnp.int32), block.astype(jnp.int32), damping


def air_kernel(
    dims, wave_ref, block_ref, table_ref, start_ref, skin_ref, skew_ref, bulk_ref, weight_ref,
    damping_ref, end_ref, flux_ref, packed, state, scaled, damped, sem,
):
    fields, levels, columns, steps, tiles = dims
    lat_count = state.shape[1]
    rows = state.shape[0]

    def tile_copy(i):
        return pltpu.make_async_copy(
            table_ref.at[wave_ref[i], :, pl.ds(pl.multiple_of(block_ref[i] * LANES, LANES), LANES)],
            packed.at[:, pl.ds(i * LANES, LANES)],
            sem.at[i],
        )

    for i in range(tiles):
        tile_copy(i).start()
    state[...] = start_ref[...].astype(jnp.float32)
    scaled[...] = (state[...] * weight_ref[...]).astype(jnp.bfloat16)
    for i in range(tiles):
        tile_copy(i).wait()

    def step(k, carry):
        for n in range(0, tiles * LANES, WIDE):
            width = min(WIDE, tiles * LANES - n)
            spectral = jnp.dot(
                scaled[...], packed[:, n : n + width], preferred_element_type=jnp.float32
            )
            factor = damping_ref[:, n : n + width]
            spectral = spectral.reshape(rows // columns, columns, width) * factor[None]
            damped[:, n : n + width] = spectral.reshape(rows, width).astype(jnp.bfloat16)
        for g in range(0, lat_count, WIDE):
            synthesis = lax.dot_general(
                damped[...],
                packed[g : g + WIDE, :],
                (((1,), (1,)), ((), ())),
                preferred_element_type=jnp.float32,
            )
            for h in range(0, WIDE, LANES):
                lanes = slice(g + h, g + h + LANES)
                flux_parts = []
                for f in range(fields):
                    middle = []
                    for l in range(levels):
                        row = (f * levels + l) * columns
                        middle.append(
                            state[row : row + columns, lanes]
                            - synthesis[row : row + columns, h : h + LANES]
                        )
                    heat = skin_ref[k, f * columns : (f + 1) * columns, lanes].astype(jnp.float32)
                    flux = bulk_ref[f : f + 1, lanes] * (heat - middle[levels - 1])
                    flux_parts.append(flux)
                    total = [mixing_diagonal * value for value in middle]
                    total[levels - 1] = total[levels - 1] + flux
                    pair = f * (levels * (levels - 1) // 2)
                    for l in range(levels):
                        for p in range(l + 1, levels):
                            skew = skew_ref[pair : pair + 1, lanes]
                            total[l] = total[l] + skew * middle[p]
                            total[p] = total[p] - skew * middle[l]
                            pair += 1
                    for l in range(levels):
                        row = (f * levels + l) * columns
                        state[row : row + columns, lanes] = total[l]
                flux_ref[k, :, lanes] = jnp.concatenate(flux_parts, axis=0).astype(jnp.bfloat16)
        scaled[...] = (state[...] * weight_ref[...]).astype(jnp.bfloat16)
        return carry

    lax.fori_loop(0, steps, step, 0)
    end_ref[...] = state[...].astype(jnp.bfloat16)


def ocean_kernel(
    dims, skew_ref, ocean_ref, damping_ref, flux_ref, basis_ref, end_ref, coef_ref, state, inverse
):
    fields, rows, steps = dims
    lon_count = ocean_ref.shape[1]
    column_count = basis_ref.shape[0]
    inverse[...] = 1.0 / (1.0 + ocean_step * damping_ref[...])
    state[...] = ocean_ref[...]

    def step(k, carry):
        forcing = jnp.dot(flux_ref[k], basis_ref[...], preferred_element_type=jnp.float32)
        forcing = forcing * (1.0 / math.sqrt(column_count))
        coarse = state[...].astype(jnp.bfloat16).astype(jnp.float32)
        coarse = coarse.reshape(fields, rows, lon_count)
        coupled = []
        for f in range(fields):
            total = skew_ref[f, 0] * coarse[0]
            for e in range(1, fields):
                total = total + skew_ref[f, e] * coarse[e]
            coupled.append(total)
        coupled = jnp.stack(coupled).reshape(fields * rows, lon_count)
        updated = (state[...] + ocean_step * (coupled - forcing)) * inverse[...]
        state[...] = updated
        coef = lax.dot_general(
            updated.astype(jnp.bfloat16),
            basis_ref[...],
            (((1,), (1,)), ((), ())),
            preferred_element_type=jnp.float32,
        )
        coef_ref[k] = (coef * (1.0 / math.sqrt(lon_count))).astype(jnp.bfloat16)
        return carry

    lax.fori_loop(0, steps, step, 0)
    end_ref[...] = state[...]


def vmem():
    return pl.BlockSpec(memory_space=pltpu.VMEM)


def smem():
    return pl.BlockSpec(memory_space=pltpu.SMEM)


def per_device(
    air_fourier_coefficients,
    quadrature_factor,
    associated_polynomial_table,
    east_west_harmonic,
    boundary_diffusion,
    bulk_transfer_coefficient,
    skin_heat_earlier,
    sea_boundary_values,
    sea_damping_speed,
    sea_coupling_matrix,
    patch_active_entries,
    sea_southern_parallel,
    sea_northern_share,
    air_paired_cells,
    air_second_share,
):
    band_index = lax.axis_index("band")
    bands = lax.axis_size("band")
    levs = lax.axis_size("lev")
    fields, levels, lat_local, column_total = air_fourier_coefficients.shape
    steps = skin_heat_earlier.shape[0]
    owned, lat_count, degree_count = associated_polynomial_table.shape
    columns = 2 * owned
    slot_rows = sea_boundary_values.shape[1]
    lon_count = sea_boundary_values.shape[2]
    all_fields = fields * levs
    part_rows = slot_rows // levs
    wave_values = lax.dynamic_slice_in_dim(east_west_harmonic, band_index * owned, owned, 0)
    tiles = (owned // 2) * (degree_count // LANES + 1)

    air_rows = fields * levels
    outgoing = jnp.concatenate(
        [
            air_fourier_coefficients.reshape(air_rows, lat_local, column_total),
            skin_heat_earlier.reshape(steps * fields, lat_local, column_total),
        ]
    ).astype(jnp.bfloat16)
    arrived = lax.all_to_all(
        outgoing.transpose(0, 2, 1), "band", split_axis=1, concat_axis=2, tiled=True
    )
    air_start = arrived[:air_rows].reshape(air_rows * columns, lat_count)
    skin = arrived[air_rows:].reshape(steps, fields * columns, lat_count)

    skew = boundary_diffusion - jnp.transpose(boundary_diffusion, (0, 2, 1, 3))
    skew = jnp.concatenate([skew[:, l, l + 1 :] for l in range(levels - 1)], axis=1)
    skew = skew.reshape(-1, lat_local).astype(jnp.bfloat16)
    skew = lax.all_gather(skew, "band", axis=1, tiled=True).astype(jnp.float32)

    live_slot = jnp.arange(slot_rows, dtype=jnp.int32) < patch_active_entries[0]
    low_tap = jnp.where(live_slot, 1.0 - sea_northern_share, 0.0)
    high_tap = jnp.where(live_slot, sea_northern_share, 0.0)
    small = jnp.concatenate(
        [
            quadrature_factor * (1.0 / math.sqrt(lat_count)),
            bulk_transfer_coefficient.reshape(-1),
            low_tap,
            high_tap,
            sea_southern_parallel.astype(jnp.float32),
        ]
    )
    small = lax.all_gather(small, "band", axis=0, tiled=False)
    near = (1 + fields) * lat_local
    weight = small[:, :lat_local].reshape(1, lat_count)
    bulk = small[:, lat_local:near].reshape(bands, fields, lat_local)
    bulk = bulk.transpose(1, 0, 2).reshape(fields, lat_count)
    low_all = small[:, near : near + slot_rows].reshape(-1).astype(jnp.bfloat16)
    high_all = small[:, near + slot_rows : near + 2 * slot_rows].reshape(-1).astype(jnp.bfloat16)
    lower = small[:, near + 2 * slot_rows :].reshape(-1).astype(jnp.int32)
    latitude = jnp.arange(lat_count, dtype=jnp.int32)[:, None]
    zero = jnp.zeros((), jnp.bfloat16)
    flux_taps = jnp.where(latitude == lower[None, :], low_all[None, :], zero) + jnp.where(
        latitude == lower[None, :] + 1, high_all[None, :], zero
    )

    sea = jnp.stack([sea_boundary_values, sea_damping_speed])
    sea = lax.all_to_all(sea, "lev", split_axis=2, concat_axis=1, tiled=True)
    sea = sea.reshape(2, all_fields * part_rows, lon_count)

    tile_wave, tile_block, damping = live_tiles(wave_values, degree_count, tiles)
    damping = damping * (1.0 / (synth_divisor * math.sqrt(degree_count)))
    rows = air_rows * columns
    air_end, flux = pl.pallas_call(
        functools.partial(air_kernel, (fields, levels, columns, steps, tiles)),
        out_shape=(
            jax.ShapeDtypeStruct((rows, lat_count), jnp.bfloat16),
            jax.ShapeDtypeStruct((steps, fields * columns, lat_count), jnp.bfloat16),
        ),
        in_specs=[smem(), smem(), pl.BlockSpec(memory_space=pl.ANY)] + [vmem()] * 6,
        out_specs=(vmem(), vmem()),
        scratch_shapes=[
            pltpu.VMEM((lat_count, tiles * LANES), jnp.bfloat16),
            pltpu.VMEM((rows, lat_count), jnp.float32),
            pltpu.VMEM((rows, lat_count), jnp.bfloat16),
            pltpu.VMEM((rows, tiles * LANES), jnp.bfloat16),
            pltpu.SemaphoreType.DMA((tiles,)),
        ],
        compiler_params=pltpu.CompilerParams(vmem_limit_bytes=VMEM_LIMIT),
        cost_estimate=pl.CostEstimate(
            flops=4 * steps * rows * lat_count * tiles * LANES,
            bytes_accessed=2 * lat_count * tiles * LANES,
            transcendentals=0,
        ),
        name="air_march",
    )(
        tile_wave, tile_block, associated_polynomial_table, air_start, skin, skew, bulk, weight,
        damping,
    )

    returned = lax.all_to_all(
        air_end.reshape(air_rows, columns, lat_count), "band", split_axis=2, concat_axis=1, tiled=True
    )
    air_coefficients_end = (
        returned.transpose(0, 2, 1)
        .reshape(fields, levels, lat_local, column_total)
        .astype(jnp.float32)
    )

    ocean_flux = jnp.dot(
        flux.reshape(steps * fields * columns, lat_count),
        flux_taps,
        preferred_element_type=jnp.float32,
    ).astype(jnp.bfloat16)
    ocean_flux = ocean_flux.reshape(steps, fields, columns, bands * levs, part_rows)
    ocean_flux = ocean_flux.transpose(3, 0, 1, 4, 2)
    ocean_flux = lax.all_to_all(
        ocean_flux, ("band", "lev"), split_axis=0, concat_axis=0, tiled=True
    )
    ocean_flux = ocean_flux.reshape(bands, levs, steps, fields, part_rows, columns)
    ocean_flux = ocean_flux.transpose(2, 1, 3, 4, 0, 5)
    ocean_flux = ocean_flux.reshape(steps, all_fields * part_rows, column_total)

    zonal_basis = zonal_table(east_west_harmonic, lon_count)
    skew_full = sea_coupling_matrix - sea_coupling_matrix.T
    sea_rows = all_fields * part_rows
    sea_end, ocean_coef = pl.pallas_call(
        functools.partial(ocean_kernel, (all_fields, part_rows, steps)),
        out_shape=(
            jax.ShapeDtypeStruct((sea_rows, lon_count), jnp.float32),
            jax.ShapeDtypeStruct((steps, sea_rows, column_total), jnp.bfloat16),
        ),
        in_specs=[smem()] + [vmem()] * 4,
        out_specs=(vmem(), vmem()),
        scratch_shapes=[pltpu.VMEM((sea_rows, lon_count), jnp.float32)] * 2,
        compiler_params=pltpu.CompilerParams(vmem_limit_bytes=VMEM_LIMIT),
        cost_estimate=pl.CostEstimate(
            flops=4 * steps * sea_rows * lon_count * column_total,
            bytes_accessed=12 * sea_rows * lon_count,
            transcendentals=0,
        ),
        name="ocean_march",
    )(skew_full, sea[0], sea[1], ocean_flux, zonal_basis)

    sea_values_end = lax.all_to_all(
        sea_end.reshape(all_fields, part_rows, lon_count), "lev", split_axis=0, concat_axis=1, tiled=True
    )
    ocean_coef = ocean_coef.reshape(steps, all_fields, part_rows, column_total)
    ocean_coef = lax.all_to_all(ocean_coef, "lev", split_axis=1, concat_axis=2, tiled=True)
    up = [(i, i + 1) for i in range(bands - 1)]
    down = [(j, i) for i, j in up]
    before = lax.ppermute(ocean_coef, "band", up)
    after = lax.ppermute(ocean_coef, "band", down)
    neighbours = jnp.concatenate([before, ocean_coef, after], axis=2)
    base_slot = (band_index - 1) * slot_rows
    slot_index = jnp.arange(3 * slot_rows, dtype=jnp.int32)[None, :]
    first_local = (air_paired_cells[0] - base_slot)[:, None]
    second_local = (air_paired_cells[1] - base_slot)[:, None]
    return_taps = jnp.where(
        slot_index == first_local, (1.0 - air_second_share)[:, None], 0.0
    ) + jnp.where(slot_index == second_local, air_second_share[:, None], 0.0)
    return_taps = return_taps.astype(jnp.bfloat16)
    skin_heat_newest = jnp.einsum(
        "ga,kfac->kfgc", return_taps, neighbours, preferred_element_type=jnp.float32
    )
    return (air_coefficients_end, sea_values_end, skin_heat_newest)


def solution(mesh):
    return jax.shard_map(
        per_device,
        mesh=mesh,
        in_specs=(
            P("lev", None, "band", None),
            P("band"),
            P("band", None, None),
            P(),
            P("lev", None, None, "band"),
            P("lev", "band"),
            P(None, "lev", "band", None),
            P("lev", "band", None),
            P("lev", "band", None),
            P(),
            P("band"),
            P("band"),
            P("band"),
            P(None, "band"),
            P("band"),
        ),
        out_specs=(
            P("lev", None, "band", None),
            P("lev", "band", None),
            P(None, "lev", "band", None),
        ),
        check_vma=False,
    )
```

time: 1310 us -> 317 us (0.24)
  waiting for transfers between devices: 501 us -> 54.3 us
  local copies, waits for them, and re-layouts: 316 us -> 56.6 us
  matrix products: 218 us -> 2.04 us
  starting transfers between devices: 146 us -> 32.3 us
  Pallas kernels: 0 us -> 71.3 us
  other arithmetic: 48.1 us -> 10.3 us
  blocking collectives: 69.7 us -> 85.7 us
    all_to_all x24 -> x5, waiting for transfers between devices: 495 us -> 44.1 us  [the longest x1 36.9 us: per_device(): lax.all_to_all(outgoing.transpose(0, 2, 1), 'band', split_axis=1, concat_...]
    dot_general x38 -> x1, matrix products: 217 us -> 0.75 us  [per_device(): jnp.dot(flux.reshape(steps * fields * columns, lat_count), flux_taps, pre...]
    all_to_all x24 -> x5, starting transfers between devices: 120 us -> 25.8 us  [the longest x1 6.94 us: per_device(): lax.all_to_all(outgoing.transpose(0, 2, 1), 'band', split_axis=1, concat_...]
    pallas_call x0 -> x2, Pallas kernels: none -> 71.3 us  [the longest x1 65 us: per_device(): pl.pallas_call(functools.partial(air_kernel, (fields, levels, columns, st...]
    convert_element_type x36 -> x6, local copies, waits for them, and re-layouts: 68.3 us -> 4 us  [the longest x2 3.66 us: per_device(): air_coefficients_end = returned.transpose(0, 2, 1).reshape(fields, levels...]
    while x97 -> x0, local copies, waits for them, and re-layouts: 63.8 us -> none
    scatter-add x12 -> x0, local copies, waits for them, and re-layouts: 56.3 us -> none  [march_air_model(): mixed_state = mixed_state.at[:, height_pile - 1].add(bottom_sheet)]
    reshape x36 -> x12, local copies, waits for them, and re-layouts: 68.9 us -> 13.8 us  [the longest x2 3.89 us: per_device(): ocean_flux = ocean_flux.reshape(steps, all_fields * part_rows, column_total)]
  transfers between devices with their start and end apart: 28 -> 7, of which waited for: 26 -> 3; matrix products, arithmetic and copies ran while one was open for 0% -> 9% of each run, Pallas kernels for 0% -> 0%
where the time goes in v1:
time: 317 us; the launch traced here: 315 us
  blocking collectives  85.7 us (27%)
  Pallas kernels  71.3 us (22%)
  local copies, waits for them, and re-layouts  56.6 us (18%)
  waiting for transfers between devices  54.3 us (17%)
  starting transfers between devices  32.3 us (10%)
  other arithmetic  10.3 us (3%)
    pallas_call x1, Pallas kernels, per_device(): pl.pallas_call(functools.partial(air_kernel, (fields, levels, columns, st...  65 us
    unnamed x1, blocking collectives  44.6 us
    all_to_all x1, waiting for transfers between devices, per_device(): lax.all_to_all(outgoing.transpose(0, 2, 1), 'band', split_axis=1, concat_...  36.9 us
    all_gather x1, blocking collectives, per_device(): skew = lax.all_gather(skew, 'band', axis=1, tiled=True).astype(jnp.float32)  34 us
    unnamed x41, local copies, waits for them, and re-layouts  14.2 us
    ppermute x1, waiting for transfers between devices, per_device(): after = lax.ppermute(ocean_coef, 'band', down)  10.2 us
    all_to_all x1, waiting for transfers between devices, per_device(): lax.all_to_all(ocean_flux, ('band', 'lev'), split_axis=0, concat_axis=0,...  7.14 us
    all_to_all x1, blocking collectives, per_device(): lax.all_to_all(ocean_coef, 'lev', split_axis=1, concat_axis=2, tiled=True)  7 us
  transfers between devices with their start and end apart: 7, of which 3 were waited for; matrix products, arithmetic and copies ran while one was open for 9% of the time, Pallas kernels for 0%

profile of v1, /device:TPU:11, one launch (start us, length us, event | category | flops | bytes accessed | tf_op | source)
XLA Modules:
  0.0 315.1 jit_solution(4476294934858421568)
XLA Ops:
  3.7 3.5 %all-to-all-start.2 = ((f32[2,2,32,1440]{3,1,0,2:T(2,128)}), f32[2,2,32,1440]{3,1,0,2:T(2,128)S(1)}, u32[]{:S(2)}, u32[]{:S(2)}) async-start(f32[2,2,32,1440]{3,1,0,2:T(2,128)} %pad_maximum_fusion), calls=%async_computation.2 | async-start | bytes 1572864 | tf_op jit(solution)/shard_map/all_to_all | solution.py:244
  10.0 44.6 %all-reduce = f32[5376]{0:T(1024)S(1)} all-reduce(f32[5376]{0:T(1024)S(1)} %dynamic-update-slice), channel_id=2, replica_groups=mesh['band'=16,'lev'=2] {'band'}, use_global_device_ids=true, to_apply=%add | all-reduce | flops 5376 | bytes 43008
  54.9 2.5 cosine_convert_fusion
  66.2 34.0 %all_gather.9 = bf16[240,1280]{0,1:T(8,128)(2,1)S(1)} all-gather(bf16[240,80]{0,1:T(8,128)(2,1)S(1)} %copy.155), channel_id=1, replica_groups=mesh['band'=16,'lev'=2] {'band'}, dimensions={1}, use_global_device_ids=true | all-gather | bytes 652800 | tf_op jit(solution)/shard_map/all_gather | solution.py:215
  100.3 6.9 %all-to-all-start = ((bf16[56,128,80]{2,0,1:T(8,128)(2,1)}), bf16[56,128,80]{2,0,1:T(8,128)(2,1)}, u32[]{:S(2)}, u32[]{:S(2)}) async-start(bf16[56,128,80]{2,0,1:T(8,128)(2,1)} %maximum_bitcast_fusion), calls=%async_computation | async-start | bytes 3670016 | tf_op jit(solution)/shard_map/all_to_all | solution.py:206
  112.2 36.9 %all-to-all-done = bf16[56,128,80]{2,0,1:T(8,128)(2,1)} async-done(((bf16[56,128,80]{2,0,1:T(8,128)(2,1)}), bf16[56,128,80]{2,0,1:T(8,128)(2,1)}, u32[]{:S(2)}, u32[]{:S(2)}) %all-to-all-start) | async-done | bytes 1146912 | tf_op jit(solution)/shard_map/all_to_all | solution.py:206
  156.6 65.0 %air_march.1 = (bf16[256,1280]{1,0:T(8,128)(2,1)S(1)}, bf16[12,16,1280]{2,1,0:T(8,128)(2,1)S(1)}) custom-call(s32[22]{0:T(128)S(1)} %broadcast_minimum_fusion.wave_ref, s32[22]{0:T(128)S(1)} %get-tuple-element.42.block_ref, bf16[4,1280,1280]{2,1,0:T(8,128)(2,1)} %table_ref.1, bf16[256,1280]{1,0:T(8,128)(2,1)} %reshape.264.start_ref, ...), custom_call_target="tpu_custom_call" | custom-call | flops 44291850240 | bytes 7208960 | tf_op jit(solution)/shard_map/air_march/pallas_call | solution.py:250
  222.3 2.4 reshape.272
  224.8 3.2 %copy.166 = bf16[32,12,2,16,8]{3,4,2,1,0:T(8,128)(2,1)} copy(bf16[32,12,2,16,8]{3,0,4,2,1:T(8,128)(2,1)} %bitcast.127) | data formatting | bytes 393216 | tf_op jit(solution)/shard_map/transpose | solution.py:292
  227.9 3.8 %reshape.295 = bf16[32,2,1536]{2,1,0:T(2,128)(2,1)} reshape(bf16[32,12,2,8,16]{4,3,2,1,0:T(8,128)(2,1)} %bitcast.128) | data formatting | bytes 393216
  231.8 4.8 %all-to-all-start.3 = ((bf16[32,2,1536]{2,1,0:T(2,128)(2,1)}), bf16[32,2,1536]{2,1,0:T(2,128)(2,1)S(1)}, u32[]{:S(2)}, u32[]{:S(2)}) async-start(bf16[32,2,1536]{2,1,0:T(2,128)(2,1)} %reshape.295), calls=%async_computation.3 | async-start | bytes 393216 | tf_op jit(solution)/shard_map/all_to_all | solution.py:293
  236.7 7.1 %all-to-all-done.3 = bf16[32,2,1536]{2,1,0:T(2,128)(2,1)S(1)} async-done(((bf16[32,2,1536]{2,1,0:T(2,128)(2,1)}), bf16[32,2,1536]{2,1,0:T(2,128)(2,1)S(1)}, u32[]{:S(2)}, u32[]{:S(2)}) %all-to-all-start.3) | async-done | bytes 196640 | tf_op jit(solution)/shard_map/all_to_all | solution.py:293
  246.1 4.2 %copy.147 = bf16[12,2,2,16,16,8]{3,2,1,5,4,0:T(2,128)(2,1)} copy(bf16[12,2,2,16,16,8]{3,5,2,0,1,4:T(8,128)(2,1)} %bitcast.129) | data formatting | bytes 393216 | tf_op jit(solution)/shard_map/transpose | solution.py:297
  250.2 3.7 %reshape.274 = bf16[12,64,128]{1,2,0:T(8,128)(2,1)S(1)} reshape(bf16[12,2,2,16,16,8]{3,2,1,5,4,0:T(2,128)(2,1)} %copy.147) | data formatting | bytes 393216 | tf_op jit(solution)/shard_map/reshape | solution.py:298
  254.1 6.3 %ocean_march.1 = (f32[64,1440]{1,0:T(8,128)}, bf16[12,64,128]{2,1,0:T(8,128)(2,1)S(1)}) custom-call(f32[4,4]{1,0:T(4,128)S(1)} %bitcast_subtract_fusion.1.skew_ref, f32[64,1440]{1,0:T(8,128)S(1)} %bitcast.118, f32[64,1440]{1,0:T(8,128)S(1)} %bitcast.117, bf16[12,64,128]{2,1,0:T(8,128)(2,1)S(1)} %copy.149.flux_ref, ...), custom_call_target="tpu_custom_call" | custom-call | flops 566231040 | bytes 1105920 | tf_op jit(solution)/shard_map/ocean_march/pallas_call | solution.py:303
  260.4 7.0 %all_to_all.83 = bf16[12,4,16,128]{3,2,0,1:T(8,128)(2,1)S(1)} all-to-all(bf16[12,4,16,128]{3,2,0,1:T(8,128)(2,1)S(1)} %copy.151), channel_id=1, replica_groups=mesh['band'=16,'lev'=2] {'lev'}, dimensions={1} | all-to-all | bytes 393216 | tf_op jit(solution)/shard_map/all_to_all | solution.py:325
  267.4 4.2 %all-to-all-start.4 = ((f32[4,16,1440]{2,1,0:T(8,128)}), f32[4,16,1440]{2,1,0:T(8,128)}, u32[]{:S(2)}, u32[]{:S(2)}) async-start(f32[4,16,1440]{2,1,0:T(8,128)} %bitcast.47), calls=%async_computation.4 | async-start | bytes 786432 | tf_op jit(solution)/shard_map/all_to_all | solution.py:321
  271.6 3.1 copy.139
  274.7 3.2 %reshape.293 = bf16[16,2,10240]{2,1,0:T(2,128)(2,1)} reshape(bf16[1280,8,32]{2,1,0:T(8,128)(2,1)S(1)} %bitcast.121) | data formatting | bytes 1310720
  277.9 6.3 %all-to-all-start.1 = ((bf16[16,2,10240]{2,1,0:T(2,128)(2,1)}), bf16[16,2,10240]{2,1,0:T(2,128)(2,1)S(1)}, u32[]{:S(2)}, u32[]{:S(2)}) async-start(bf16[16,2,10240]{2,1,0:T(2,128)(2,1)} %reshape.293), calls=%async_computation.1 | async-start | bytes 1310720 | tf_op jit(solution)/shard_map/all_to_all | solution.py:277
  286.5 4.2 %collective-permute-start = (bf16[12,2,32,128]{3,2,1,0:T(8,128)(2,1)S(1)}, bf16[12,2,32,128]{3,2,1,0:T(8,128)(2,1)S(1)}, u32[]{:S(2)}, u32[]{:S(2)}) collective-permute-start(bf16[12,2,32,128]{3,2,1,0:T(8,128)(2,1)S(1)} %bitcast.135), channel_id=1, source_target_pairs={{0,2},{2,4},{4,6},{6,8},{8,10},{10,12},{12,14},{14,16},{16,18},{18... | collective-permute-start | bytes 589832 | tf_op jit(solution)/shard_map/ppermute | solution.py:328
  292.5 10.2 %collective-permute-done.1 = bf16[12,2,32,128]{3,2,1,0:T(8,128)(2,1)S(1)} collective-permute-done((bf16[12,2,32,128]{3,2,1,0:T(8,128)(2,1)S(1)}, bf16[12,2,32,128]{3,2,1,0:T(8,128)(2,1)S(1)}, u32[]{:S(2)}, u32[]{:S(2)}) %collective-permute-start.1) | collective-permute-done | bytes 196640 | tf_op jit(solution)/shard_map/ppermute | solution.py:329
  305.3 3.4 %copy.140 = bf16[32,8,1280]{2,1,0:T(8,128)(2,1)S(1)} copy(bf16[32,8,1280]{0,1,2:T(8,128)(2,1)S(1)} %bitcast.122) | data formatting | bytes 1310720 | tf_op jit(solution)/shard_map/all_to_all | solution.py:277
  312.4 2.7 copy.153
  (127 shorter events, 39.1 us)
Async XLA Ops:
  2.4 4.9 %copy-start.4 = (f32[2,16,16,80]{3,2,1,0:T(8,128)S(1)}, f32[2,16,16,80]{3,2,1,0:T(8,128)}, u32[]{:S(2)}) copy-start(f32[2,16,16,80]{3,2,1,0:T(8,128)} %param.19) | copy-start | bytes 491524
  2.4 5.2 %copy-start.11 = (f32[80]{0:T(128)S(1)}, f32[80]{0:T(128)}, u32[]{:S(2)}) copy-start(f32[80]{0:T(128)} %param.16) | copy-start | bytes 964
  2.4 5.2 %copy-start.7 = (f32[2,80]{1,0:T(2,128)S(1)}, f32[2,80]{1,0:T(2,128)}, u32[]{:S(2)}) copy-start(f32[2,80]{1,0:T(2,128)} %param.20) | copy-start | bytes 1924
  2.4 6.0 %copy-start.12 = (s32[32]{0:T(128)S(1)}, s32[32]{0:T(128)}, u32[]{:S(2)}) copy-start(s32[32]{0:T(128)} %param.26) | copy-start | bytes 388
  2.4 6.0 %copy-start.10 = (f32[32]{0:T(128)S(1)}, f32[32]{0:T(128)}, u32[]{:S(2)}) copy-start(f32[32]{0:T(128)} %param.27) | copy-start | bytes 388
  2.4 6.0 %copy-start.15 = (u32[32]{0:T(128)S(1)}, u32[32]{0:T(128)}, u32[]{:S(2)}) copy-start(u32[32]{0:T(128)} %constant.81) | copy-start | bytes 388
  2.4 52.4 %copy-start.6 = (s32[64]{0:T(128)S(1)}, s32[64]{0:T(128)}, u32[]{:S(2)}) copy-start(s32[64]{0:T(128)} %param.18) | copy-start | bytes 772
  2.4 55.9 %copy-start.1 = (f32[12,2,80,128]{3,2,1,0:T(8,128)S(1)}, f32[12,2,80,128]{3,2,1,0:T(8,128)}, u32[]{:S(2)}) copy-start(f32[12,2,80,128]{3,2,1,0:T(8,128)} %param.21) | copy-start | bytes 2949124
  3.7 96.6 %all-to-all-start.2 = ((f32[2,2,32,1440]{3,1,0,2:T(2,128)}), f32[2,2,32,1440]{3,1,0,2:T(2,128)S(1)}, u32[]{:S(2)}, u32[]{:S(2)}) async-start(f32[2,2,32,1440]{3,1,0,2:T(2,128)} %pad_maximum_fusion), calls=%async_computation.2 | async-start | bytes 1572864 | tf_op jit(solution)/shard_map/all_to_all | solution.py:244
  54.8 53.2 %copy-start.3 = (f32[16,336]{1,0:T(8,128)}, f32[16,336]{1,0:T(8,128)S(1)}, u32[]{:S(2)}) copy-start(f32[16,336]{1,0:T(8,128)S(1)} %reshape.285) | copy-start | bytes 64516
  57.6 0.8 copy-start.13
  59.1 5.5 %copy-start.2 = (bf16[64,1,1440]{2,0,1:T(8,128)(2,1)S(1)}, bf16[64,1,1440]{2,0,1:T(8,128)(2,1)}, u32[]{:S(2)}) copy-start(bf16[64,1,1440]{2,0,1:T(8,128)(2,1)} %get-tuple-element.40) | copy-start | bytes 552964
  100.3 48.9 %all-to-all-start = ((bf16[56,128,80]{2,0,1:T(8,128)(2,1)}), bf16[56,128,80]{2,0,1:T(8,128)(2,1)}, u32[]{:S(2)}, u32[]{:S(2)}) async-start(bf16[56,128,80]{2,0,1:T(8,128)(2,1)} %maximum_bitcast_fusion), calls=%async_computation | async-start | bytes 3670016 | tf_op jit(solution)/shard_map/all_to_all | solution.py:206
  107.2 2.5 copy-start.5
  108.0 1.5 slice-start
  108.2 2.5 copy-start.14
  227.9 8.7 %copy-start = (f32[2,2,2,16,1440]{4,3,1,2,0:T(8,128)S(1)}, f32[2,2,2,16,1440]{4,3,1,2,0:T(8,128)}, u32[]{:S(2)}) copy-start(f32[2,2,2,16,1440]{4,3,1,2,0:T(8,128)} %copy.164) | copy-start | bytes 2211844
  231.8 12.1 %all-to-all-start.3 = ((bf16[32,2,1536]{2,1,0:T(2,128)(2,1)}), bf16[32,2,1536]{2,1,0:T(2,128)(2,1)S(1)}, u32[]{:S(2)}, u32[]{:S(2)}) async-start(bf16[32,2,1536]{2,1,0:T(2,128)(2,1)} %reshape.295), calls=%async_computation.3 | async-start | bytes 393216 | tf_op jit(solution)/shard_map/all_to_all | solution.py:293
  267.4 10.4 %all-to-all-start.4 = ((f32[4,16,1440]{2,1,0:T(8,128)}), f32[4,16,1440]{2,1,0:T(8,128)}, u32[]{:S(2)}, u32[]{:S(2)}) async-start(f32[4,16,1440]{2,1,0:T(8,128)} %bitcast.47), calls=%async_computation.4 | async-start | bytes 786432 | tf_op jit(solution)/shard_map/all_to_all | solution.py:321
  274.7 9.5 %copy-start.8 = (s32[2,80]{1,0:T(2,128)S(1)}, s32[2,80]{1,0:T(2,128)}, u32[]{:S(2)}) copy-start(s32[2,80]{1,0:T(2,128)} %param.28) | copy-start | bytes 1924
  274.7 16.0 %copy-start.9 = (f32[80]{0:T(128)S(1)}, f32[80]{0:T(128)}, u32[]{:S(2)}) copy-start(f32[80]{0:T(128)} %param.29) | copy-start | bytes 964
  277.9 26.2 %all-to-all-start.1 = ((bf16[16,2,10240]{2,1,0:T(2,128)(2,1)}), bf16[16,2,10240]{2,1,0:T(2,128)(2,1)S(1)}, u32[]{:S(2)}, u32[]{:S(2)}) async-start(bf16[16,2,10240]{2,1,0:T(2,128)(2,1)} %reshape.293), calls=%async_computation.1 | async-start | bytes 1310720 | tf_op jit(solution)/shard_map/all_to_all | solution.py:277
  284.3 18.5 %collective-permute-start.1 = (bf16[12,2,32,128]{3,2,1,0:T(8,128)(2,1)S(1)}, bf16[12,2,32,128]{3,2,1,0:T(8,128)(2,1)S(1)}, u32[]{:S(2)}, u32[]{:S(2)}) collective-permute-start(bf16[12,2,32,128]{3,2,1,0:T(8,128)(2,1)S(1)} %bitcast.134), channel_id=1, source_target_pairs={{2,0},{4,2},{6,4},{8,6},{10,8},{12,10},{14,12},{16,14},{18,16},{20... | collective-permute-start | bytes 589832 | tf_op jit(solution)/shard_map/ppermute | solution.py:329
  286.5 16.2 %collective-permute-start = (bf16[12,2,32,128]{3,2,1,0:T(8,128)(2,1)S(1)}, bf16[12,2,32,128]{3,2,1,0:T(8,128)(2,1)S(1)}, u32[]{:S(2)}, u32[]{:S(2)}) collective-permute-start(bf16[12,2,32,128]{3,2,1,0:T(8,128)(2,1)S(1)} %bitcast.135), channel_id=1, source_target_pairs={{0,2},{2,4},{4,6},{6,8},{8,10},{10,12},{12,14},{14,16},{16,18},{18... | collective-permute-start | bytes 589832 | tf_op jit(solution)/shard_map/ppermute | solution.py:328

commit v2 on v1

--- a/solution.py
+++ b/solution.py
@@ -49,13 +49,65 @@
     return wave.astype(jnp.int32), block.astype(jnp.int32), damping
 
 
+def regroup(read, group, sources, width):
+    lane_block = None
+    total = None
+    offset = group * width
+    tile = pl.ds(pl.multiple_of(offset // LANES * LANES, LANES), LANES)
+    for place, source in enumerate(sources):
+        piece = read(source, tile).astype(jnp.float32)
+        shift = lax.rem(place * width - lax.rem(offset, LANES) + LANES, LANES)
+        piece = pltpu.roll(piece, shift, 1)
+        if total is None:
+            lane_block = lax.broadcasted_iota(jnp.int32, piece.shape, 1) // width
+            total = jnp.where(lane_block == place, piece, 0.0)
+        else:
+            total = jnp.where(lane_block == place, piece, total)
+    return total
+
+
+def pack_kernel(columns, air_ref, skin_ref, out_ref):
+    air_rows = air_ref.shape[0]
+    used = air_rows + skin_ref.shape[0]
+    per_tile = LANES // columns
+
+    def read(row, tile):
+        return air_ref[row, :, tile] if row < air_rows else skin_ref[row - air_rows, :, tile]
+
+    def one(band, carry):
+        for t in range(out_ref.shape[2] // LANES):
+            sources = range(t * per_tile, min((t + 1) * per_tile, used))
+            out_ref[band, :, t * LANES : (t + 1) * LANES] = regroup(
+                read, band, sources, columns
+            ).astype(out_ref.dtype)
+        return carry
+
+    lax.fori_loop(0, out_ref.shape[0], one, 0)
+
+
+def unpack_kernel(columns, in_ref, out_ref):
+    per_tile = LANES // columns
+
+    def one(row, carry):
+        for t in range(out_ref.shape[2] // LANES):
+            out_ref[row, :, t * LANES : (t + 1) * LANES] = regroup(
+                lambda band, tile: in_ref[band, :, tile],
+                row,
+                range(t * per_tile, (t + 1) * per_tile),
+                columns,
+            )
+        return carry
+
+    lax.fori_loop(0, out_ref.shape[0], one, 0)
+
+
 def air_kernel(
-    dims, wave_ref, block_ref, table_ref, start_ref, skin_ref, skew_ref, bulk_ref, weight_ref,
+    dims, wave_ref, block_ref, table_ref, start_ref, skew_ref, bulk_ref, weight_ref,
     damping_ref, end_ref, flux_ref, packed, state, scaled, damped, sem,
 ):
     fields, levels, columns, steps, tiles = dims
     lat_count = state.shape[1]
-    rows = state.shape[0]
+    rows = fields * levels * columns
 
     def tile_copy(i):
         return pltpu.make_async_copy(
@@ -66,8 +118,11 @@
 
     for i in range(tiles):
         tile_copy(i).start()
-    state[...] = start_ref[...].astype(jnp.float32)
-    scaled[...] = (state[...] * weight_ref[...]).astype(jnp.bfloat16)
+    for g in range(0, lat_count, LANES):
+        for r in range(0, state.shape[0], LANES):
+            block = start_ref[g : g + LANES, r : r + LANES].astype(jnp.float32)
+            state[r : r + LANES, g : g + LANES] = block.T
+    scaled[...] = (state[:rows] * weight_ref[...]).astype(jnp.bfloat16)
     for i in range(tiles):
         tile_copy(i).wait()
 
@@ -98,7 +153,8 @@
                             state[row : row + columns, lanes]
                             - synthesis[row : row + columns, h : h + LANES]
                         )
-                    heat = skin_ref[k, f * columns : (f + 1) * columns, lanes].astype(jnp.float32)
+                    heat_row = rows + k * (fields * columns) + f * columns
+                    heat = state[pl.ds(pl.multiple_of(heat_row, columns), columns), lanes]
                     flux = bulk_ref[f : f + 1, lanes] * (heat - middle[levels - 1])
                     flux_parts.append(flux)
                     total = [mixing_diagonal * value for value in middle]
@@ -114,24 +170,44 @@
                         row = (f * levels + l) * columns
                         state[row : row + columns, lanes] = total[l]
                 flux_ref[k, :, lanes] = jnp.concatenate(flux_parts, axis=0).astype(jnp.bfloat16)
-        scaled[...] = (state[...] * weight_ref[...]).astype(jnp.bfloat16)
+        scaled[...] = (state[:rows] * weight_ref[...]).astype(jnp.bfloat16)
         return carry
 
     lax.fori_loop(0, steps, step, 0)
-    end_ref[...] = state[...].astype(jnp.bfloat16)
+    for g in range(0, lat_count, LANES):
+        for r in range(0, rows, LANES):
+            block = state[r : r + LANES, g : g + LANES]
+            end_ref[g : g + LANES, r : r + LANES] = block.T.astype(jnp.bfloat16)
 
 
 def ocean_kernel(
-    dims, skew_ref, ocean_ref, damping_ref, flux_ref, basis_ref, end_ref, coef_ref, state, inverse
+    dims, skew_ref, ocean_ref, damping_ref, flux_ref, basis_ref, end_ref, coef_ref, state, inverse,
+    flux_now,
 ):
-    fields, rows, steps = dims
+    fields, own_fields, rows, steps, columns = dims
+    per_tile = LANES // columns
     lon_count = ocean_ref.shape[1]
     column_count = basis_ref.shape[0]
     inverse[...] = 1.0 / (1.0 + ocean_step * damping_ref[...])
     state[...] = ocean_ref[...]
 
     def step(k, carry):
-        forcing = jnp.dot(flux_ref[k], basis_ref[...], preferred_element_type=jnp.float32)
+        for f in range(own_fields):
+            for t in range(column_count // LANES):
+                part = regroup(
+                    lambda band, tile: flux_ref[band, :, tile],
+                    k * own_fields + f,
+                    range(t * per_tile, (t + 1) * per_tile),
+                    columns,
+                )
+                for v in range(fields // own_fields):
+                    start = (v * own_fields + f) * rows
+                    flux_now[start : start + rows, t * LANES : (t + 1) * LANES] = part[
+                        v * rows : (v + 1) * rows
+                    ]
+        forcing = jnp.dot(
+            flux_now[...].astype(jnp.bfloat16), basis_ref[...], preferred_element_type=jnp.float32
+        )
         forcing = forcing * (1.0 / math.sqrt(column_count))
         coarse = state[...].astype(jnp.bfloat16).astype(jnp.float32)
         coarse = coarse.reshape(fields, rows, lon_count)
@@ -163,6 +239,26 @@
 
 def smem():
     return pl.BlockSpec(memory_space=pltpu.SMEM)
+
+
+def lev_exchange(values, split_axis, concat_axis):
+    count = lax.axis_size("lev")
+    me = lax.axis_index("lev")
+    size = values.shape[split_axis] // count
+    pieces = []
+    for shift in range(count):
+        target = lax.rem(me + shift, count)
+        chunk = lax.dynamic_slice_in_dim(values, target * size, size, split_axis)
+        if shift:
+            chunk = lax.ppermute(chunk, "lev", [(i, (i + shift) % count) for i in range(count)])
+        pieces.append(chunk)
+    ordered = []
+    for source in range(count):
+        found = pieces[0]
+        for shift in range(1, count):
+            found = jnp.where(lax.rem(me - source + count, count) == shift, pieces[shift], found)
+        ordered.append(found)
+    return jnp.concatenate(ordered, axis=concat_axis)
 
 
 def per_device(
@@ -197,52 +293,61 @@
     tiles = (owned // 2) * (degree_count // LANES + 1)
 
     air_rows = fields * levels
-    outgoing = jnp.concatenate(
-        [
-            air_fourier_coefficients.reshape(air_rows, lat_local, column_total),
-            skin_heat_earlier.reshape(steps * fields, lat_local, column_total),
-        ]
-    ).astype(jnp.bfloat16)
-    arrived = lax.all_to_all(
-        outgoing.transpose(0, 2, 1), "band", split_axis=1, concat_axis=2, tiled=True
-    )
-    air_start = arrived[:air_rows].reshape(air_rows * columns, lat_count)
-    skin = arrived[air_rows:].reshape(steps, fields * columns, lat_count)
+    sent_lanes = -(-(air_rows + steps * fields) * columns // LANES) * LANES
+    outgoing = pl.pallas_call(
+        functools.partial(pack_kernel, columns),
+        out_shape=jax.ShapeDtypeStruct((bands, lat_local, sent_lanes), jnp.bfloat16),
+        in_specs=[vmem()] * 2,
+        out_specs=vmem(),
+        compiler_params=pltpu.CompilerParams(vmem_limit_bytes=VMEM_LIMIT),
+        name="pack_rows",
+    )(
+        air_fourier_coefficients.reshape(air_rows, lat_local, column_total),
+        skin_heat_earlier.reshape(steps * fields, lat_local, column_total),
+    )
+    arrived = lax.all_to_all(outgoing, "band", split_axis=0, concat_axis=0, tiled=True)
+    air_start = arrived.reshape(lat_count, sent_lanes)
 
     skew = boundary_diffusion - jnp.transpose(boundary_diffusion, (0, 2, 1, 3))
     skew = jnp.concatenate([skew[:, l, l + 1 :] for l in range(levels - 1)], axis=1)
     skew = skew.reshape(-1, lat_local).astype(jnp.bfloat16)
-    skew = lax.all_gather(skew, "band", axis=1, tiled=True).astype(jnp.float32)
+    pairs = skew.shape[0]
 
     live_slot = jnp.arange(slot_rows, dtype=jnp.int32) < patch_active_entries[0]
     low_tap = jnp.where(live_slot, 1.0 - sea_northern_share, 0.0)
     high_tap = jnp.where(live_slot, sea_northern_share, 0.0)
+    near = (sea_southern_parallel - band_index * lat_local).astype(jnp.float32)
+    taps = jnp.concatenate([low_tap, high_tap, near])
+    tap_rows = -(-taps.shape[0] // lat_local)
+    taps = jnp.pad(taps, (0, tap_rows * lat_local - taps.shape[0])).reshape(tap_rows, lat_local)
+    factors = jnp.concatenate(
+        [quadrature_factor[None] * (1.0 / math.sqrt(lat_count)), bulk_transfer_coefficient]
+    )
+    rounded = lax.reduce_precision(factors, exponent_bits=8, mantissa_bits=7)
     small = jnp.concatenate(
-        [
-            quadrature_factor * (1.0 / math.sqrt(lat_count)),
-            bulk_transfer_coefficient.reshape(-1),
-            low_tap,
-            high_tap,
-            sea_southern_parallel.astype(jnp.float32),
-        ]
+        [skew]
+        + [value.astype(jnp.bfloat16) for value in (rounded, factors - rounded, taps)]
     )
     small = lax.all_gather(small, "band", axis=0, tiled=False)
-    near = (1 + fields) * lat_local
-    weight = small[:, :lat_local].reshape(1, lat_count)
-    bulk = small[:, lat_local:near].reshape(bands, fields, lat_local)
-    bulk = bulk.transpose(1, 0, 2).reshape(fields, lat_count)
-    low_all = small[:, near : near + slot_rows].reshape(-1).astype(jnp.bfloat16)
-    high_all = small[:, near + slot_rows : near + 2 * slot_rows].reshape(-1).astype(jnp.bfloat16)
-    lower = small[:, near + 2 * slot_rows :].reshape(-1).astype(jnp.int32)
-    latitude = jnp.arange(lat_count, dtype=jnp.int32)[:, None]
+    by_row = small[:, : pairs + 2 * (1 + fields)].transpose(1, 0, 2).reshape(-1, lat_count)
+    by_row = by_row.astype(jnp.float32)
+    skew = by_row[:pairs]
+    factors = by_row[pairs : pairs + 1 + fields] + by_row[pairs + 1 + fields :]
+    weight = factors[:1]
+    bulk = factors[1:]
+    taps = small[:, pairs + 2 * (1 + fields) :].reshape(bands, tap_rows * lat_local)
+    low_all = taps[:, :slot_rows].reshape(-1)
+    high_all = taps[:, slot_rows : 2 * slot_rows].reshape(-1)
+    lower = taps[:, 2 * slot_rows : 3 * slot_rows].astype(jnp.int32)
+    lower = (lower + lat_local * jnp.arange(bands, dtype=jnp.int32)[:, None]).reshape(-1)
+    latitude = jnp.arange(lat_count, dtype=jnp.int32)[None, :]
     zero = jnp.zeros((), jnp.bfloat16)
-    flux_taps = jnp.where(latitude == lower[None, :], low_all[None, :], zero) + jnp.where(
-        latitude == lower[None, :] + 1, high_all[None, :], zero
+    flux_taps = jnp.where(latitude == lower[:, None], low_all[:, None], zero) + jnp.where(
+        latitude == lower[:, None] + 1, high_all[:, None], zero
     )
 
     sea = jnp.stack([sea_boundary_values, sea_damping_speed])
-    sea = lax.all_to_all(sea, "lev", split_axis=2, concat_axis=1, tiled=True)
-    sea = sea.reshape(2, all_fields * part_rows, lon_count)
+    sea = lev_exchange(sea, 2, 1).reshape(2, all_fields * part_rows, lon_count)
 
     tile_wave, tile_block, damping = live_tiles(wave_values, degree_count, tiles)
     damping = damping * (1.0 / (synth_divisor * math.sqrt(degree_count)))
@@ -250,14 +355,14 @@
     air_end, flux = pl.pallas_call(
         functools.partial(air_kernel, (fields, levels, columns, steps, tiles)),
         out_shape=(
-            jax.ShapeDtypeStruct((rows, lat_count), jnp.bfloat16),
+            jax.ShapeDtypeStruct((lat_count, rows), jnp.bfloat16),
             jax.ShapeDtypeStruct((steps, fields * columns, lat_count), jnp.bfloat16),
         ),
-        in_specs=[smem(), smem(), pl.BlockSpec(memory_space=pl.ANY)] + [vmem()] * 6,
+        in_specs=[smem(), smem(), pl.BlockSpec(memory_space=pl.ANY)] + [vmem()] * 5,
         out_specs=(vmem(), vmem()),
         scratch_shapes=[
             pltpu.VMEM((lat_count, tiles * LANES), jnp.bfloat16),
-            pltpu.VMEM((rows, lat_count), jnp.float32),
+            pltpu.VMEM((sent_lanes, lat_count), jnp.float32),
             pltpu.VMEM((rows, lat_count), jnp.bfloat16),
             pltpu.VMEM((rows, tiles * LANES), jnp.bfloat16),
             pltpu.SemaphoreType.DMA((tiles,)),
@@ -270,45 +375,52 @@
         ),
         name="air_march",
     )(
-        tile_wave, tile_block, associated_polynomial_table, air_start, skin, skew, bulk, weight,
+        tile_wave, tile_block, associated_polynomial_table, air_start, skew, bulk, weight,
         damping,
     )
 
-    returned = lax.all_to_all(
-        air_end.reshape(air_rows, columns, lat_count), "band", split_axis=2, concat_axis=1, tiled=True
-    )
-    air_coefficients_end = (
-        returned.transpose(0, 2, 1)
-        .reshape(fields, levels, lat_local, column_total)
-        .astype(jnp.float32)
-    )
-
-    ocean_flux = jnp.dot(
+    ocean_flux = lax.dot_general(
+        flux_taps,
         flux.reshape(steps * fields * columns, lat_count),
-        flux_taps,
+        (((1,), (1,)), ((), ())),
         preferred_element_type=jnp.float32,
     ).astype(jnp.bfloat16)
-    ocean_flux = ocean_flux.reshape(steps, fields, columns, bands * levs, part_rows)
-    ocean_flux = ocean_flux.transpose(3, 0, 1, 4, 2)
+    flux_lanes = -(-ocean_flux.shape[1] // LANES) * LANES
+    ocean_flux = jnp.pad(ocean_flux, ((0, 0), (0, flux_lanes - ocean_flux.shape[1])))
     ocean_flux = lax.all_to_all(
-        ocean_flux, ("band", "lev"), split_axis=0, concat_axis=0, tiled=True
-    )
-    ocean_flux = ocean_flux.reshape(bands, levs, steps, fields, part_rows, columns)
-    ocean_flux = ocean_flux.transpose(2, 1, 3, 4, 0, 5)
-    ocean_flux = ocean_flux.reshape(steps, all_fields * part_rows, column_total)
+        ocean_flux.reshape(bands * levs, part_rows, flux_lanes),
+        ("band", "lev"),
+        split_axis=0,
+        concat_axis=0,
+        tiled=True,
+    )
+    ocean_flux = ocean_flux.reshape(bands, levs * part_rows, flux_lanes)
+
+    returned = lax.all_to_all(
+        air_end.reshape(bands, lat_local, rows), "band", split_axis=0, concat_axis=0, tiled=True
+    )
+    air_coefficients_end = pl.pallas_call(
+        functools.partial(unpack_kernel, columns),
+        out_shape=jax.ShapeDtypeStruct((air_rows, lat_local, column_total), jnp.float32),
+        in_specs=[vmem()],
+        out_specs=vmem(),
+        compiler_params=pltpu.CompilerParams(vmem_limit_bytes=VMEM_LIMIT),
+        name="unpack_rows",
+    )(returned).reshape(air_fourier_coefficients.shape)
 
     zonal_basis = zonal_table(east_west_harmonic, lon_count)
     skew_full = sea_coupling_matrix - sea_coupling_matrix.T
     sea_rows = all_fields * part_rows
     sea_end, ocean_coef = pl.pallas_call(
-        functools.partial(ocean_kernel, (all_fields, part_rows, steps)),
+        functools.partial(ocean_kernel, (all_fields, fields, part_rows, steps, columns)),
         out_shape=(
             jax.ShapeDtypeStruct((sea_rows, lon_count), jnp.float32),
             jax.ShapeDtypeStruct((steps, sea_rows, column_total), jnp.bfloat16),
         ),
         in_specs=[smem()] + [vmem()] * 4,
         out_specs=(vmem(), vmem()),
-        scratch_shapes=[pltpu.VMEM((sea_rows, lon_count), jnp.float32)] * 2,
+        scratch_shapes=[pltpu.VMEM((sea_rows, lon_count), jnp.float32)] * 2
+        + [pltpu.VMEM((sea_rows, column_total), jnp.float32)],
         compiler_params=pltpu.CompilerParams(vmem_limit_bytes=VMEM_LIMIT),
         cost_estimate=pl.CostEstimate(
             flops=4 * steps * sea_rows * lon_count * column_total,
@@ -318,20 +430,34 @@
         name="ocean_march",
     )(skew_full, sea[0], sea[1], ocean_flux, zonal_basis)
 
-    sea_values_end = lax.all_to_all(
-        sea_end.reshape(all_fields, part_rows, lon_count), "lev", split_axis=0, concat_axis=1, tiled=True
-    )
+    sea_values_end = lev_exchange(
+        sea_end.reshape(all_fields, part_rows, lon_count), 0, 1
+    )
+    lev_index = lax.axis_index("lev")
     ocean_coef = ocean_coef.reshape(steps, all_fields, part_rows, column_total)
-    ocean_coef = lax.all_to_all(ocean_coef, "lev", split_axis=1, concat_axis=2, tiled=True)
-    up = [(i, i + 1) for i in range(bands - 1)]
-    down = [(j, i) for i, j in up]
-    before = lax.ppermute(ocean_coef, "band", up)
-    after = lax.ppermute(ocean_coef, "band", down)
-    neighbours = jnp.concatenate([before, ocean_coef, after], axis=2)
-    base_slot = (band_index - 1) * slot_rows
-    slot_index = jnp.arange(3 * slot_rows, dtype=jnp.int32)[None, :]
-    first_local = (air_paired_cells[0] - base_slot)[:, None]
-    second_local = (air_paired_cells[1] - base_slot)[:, None]
+    pieces, slots = [], []
+    for shift in range(levs):
+        chunk = lax.dynamic_slice_in_dim(
+            ocean_coef, lax.rem(lev_index + shift, levs) * fields, fields, 1
+        )
+        source = lax.rem(lev_index - shift + levs, levs)
+        for hop in (-1, 0, 1):
+            if hop or shift:
+                pairs_of = [
+                    (b * levs + v, (b + hop) * levs + (v + shift) % levs)
+                    for b in range(bands)
+                    for v in range(levs)
+                    if 0 <= b + hop < bands
+                ]
+                pieces.append(lax.ppermute(chunk, ("band", "lev"), pairs_of))
+            else:
+                pieces.append(chunk)
+            slots.append((band_index - hop) * slot_rows + source * part_rows)
+    neighbours = jnp.concatenate(pieces, axis=2)
+    part = jnp.arange(part_rows, dtype=jnp.int32)
+    slot_index = jnp.concatenate([slot + part for slot in slots])[None, :]
+    first_local = air_paired_cells[0][:, None]
+    second_local = air_paired_cells[1][:, None]
     return_taps = jnp.where(
         slot_index == first_local, (1.0 - air_second_share)[:, None], 0.0
     ) + jnp.where(slot_index == second_local, air_second_share[:, None], 0.0)

time: 317 us -> 193 us (0.61)
  blocking collectives: 85.7 us -> 36.3 us
  local copies, waits for them, and re-layouts: 56.6 us -> 9.5 us
  waiting for transfers between devices: 54.3 us -> 10.4 us
  Pallas kernels: 71.3 us -> 90 us
  other arithmetic: 10.3 us -> 6.8 us
    unnamed x1 -> x0, blocking collectives: 44.6 us -> none
    all_to_all x5 -> x3, waiting for transfers between devices: 44.1 us -> 7.09 us  [the longest x1 7.09 us: per_device(): lax.all_to_all(ocean_flux.reshape(bands * levs, part_rows, flux_lanes), (...]
    pallas_call x1 -> x3, Pallas kernels: 6.28 us -> 21.9 us  [the longest x1 8.39 us: per_device(): pl.pallas_call(functools.partial(pack_kernel, columns), out_shape=jax.Sha...]
    reshape x12 -> x1, local copies, waits for them, and re-layouts: 13.8 us -> 0.09 us  [per_device(): small[:, pairs + 2 * (1 + fields):].reshape(bands, tap_rows * lat_local)]
    unnamed x41 -> x31, local copies, waits for them, and re-layouts: 14.2 us -> 1.54 us
    ppermute x2 -> x7, starting transfers between devices: 6.46 us -> 16.9 us  [the longest x5 14.7 us: per_device(): pieces.append(lax.ppermute(chunk, ('band', 'lev'), pairs_of))]
    all_to_all x5 -> x0, local copies, waits for them, and re-layouts: 8.24 us -> none  [the longest x1 3.38 us: per_device(): lax.all_to_all(air_end.reshape(air_rows, columns, lat_count), 'band', spl...]
    all_to_all x5 -> x3, starting transfers between devices: 25.8 us -> 17.6 us  [the longest x1 6.7 us: per_device(): lax.all_to_all(outgoing, 'band', split_axis=0, concat_axis=0, tiled=True)]
  transfers between devices with their start and end apart: 7 -> 10, of which waited for: 3 -> 3; matrix products, arithmetic and copies ran while one was open for 9% -> 9% of each run, Pallas kernels for 0% -> 39%
where the time goes in v2:
time: 193 us; the launch traced here: 192 us
  Pallas kernels  90 us (47%)
  blocking collectives  36.3 us (19%)
  starting transfers between devices  34.5 us (18%)
  waiting for transfers between devices  10.4 us (5%)
  local copies, waits for them, and re-layouts  9.5 us (5%)
  other arithmetic  6.8 us (4%)
  matrix products  2.37 us (1%)
  between operations  1.94 us (1%)
    pallas_call x1, Pallas kernels, per_device(): pl.pallas_call(functools.partial(air_kernel, (fields, levels, columns, st...  68.1 us
    all_gather x1, blocking collectives, per_device(): small = lax.all_gather(small, 'band', axis=0, tiled=False)  36.3 us
    ppermute x5, starting transfers between devices, per_device(): pieces.append(lax.ppermute(chunk, ('band', 'lev'), pairs_of))  14.7 us
    pallas_call x1, Pallas kernels, per_device(): pl.pallas_call(functools.partial(pack_kernel, columns), out_shape=jax.Sha...  8.39 us
    pallas_call x1, Pallas kernels, per_device(): pl.pallas_call(functools.partial(ocean_kernel, (all_fields, fields, part_...  7.38 us
    all_to_all x1, waiting for transfers between devices, per_device(): lax.all_to_all(ocean_flux.reshape(bands * levs, part_rows, flux_lanes), (...  7.09 us
    all_to_all x1, starting transfers between devices, per_device(): lax.all_to_all(outgoing, 'band', split_axis=0, concat_axis=0, tiled=True)  6.7 us
    pallas_call x1, Pallas kernels, per_device(): pl.pallas_call(functools.partial(unpack_kernel, columns), out_shape=jax.S...  6.16 us
  transfers between devices with their start and end apart: 10, of which 3 were waited for; matrix products, arithmetic and copies ran while one was open for 9% of the time, Pallas kernels for 39%

profile of v2, /device:TPU:11, one launch (start us, length us, event | category | flops | bytes accessed | tf_op | source)
XLA Modules:
  0.0 191.8 jit_solution(8671219169212046657)
XLA Ops:
  0.6 1.2 copy-done
  1.8 8.4 %pack_rows.1 = bf16[16,80,512]{2,1,0:T(8,128)(2,1)} custom-call(f32[32,80,128]{2,1,0:T(8,128)} %bitcast.98, f32[24,80,128]{2,1,0:T(8,128)S(1)} %bitcast.84), custom_call_target="tpu_custom_call" | custom-call | tf_op jit(solution)/shard_map/pack_rows/pallas_call | solution.py:297
  10.2 6.7 %all-to-all-start = ((bf16[16,80,512]{2,1,0:T(8,128)(2,1)}), bf16[16,80,512]{2,1,0:T(8,128)(2,1)}, u32[]{:S(2)}, u32[]{:S(2)}) async-start(bf16[16,80,512]{2,1,0:T(8,128)(2,1)} %pack_rows.1), calls=%async_computation | async-start | bytes 2621440 | tf_op jit(solution)/shard_map/all_to_all | solution.py:308
  17.8 1.2 collective-permute-start
  20.2 1.2 concatenate.26
  22.9 36.3 %all-gather.1 = bf16[16,248,80]{1,2,0:T(8,128)(2,1)S(1)} all-gather(bf16[1,248,80]{1,2,0:T(8,128)(2,1)S(1)} %maximum_bitcast_fusion), channel_id=2, replica_groups=mesh['band'=16,'lev'=2] {'band'}, dimensions={0}, use_global_device_ids=true | all-gather | bytes 674560 | tf_op jit(solution)/shard_map/all_gather | solution.py:331
  60.5 1.8 cosine_convert_fusion
  62.8 1.4 copy.72.skew_ref
  65.4 1.0 convert_element_type.77.basis_ref
  67.7 68.1 %air_march.1 = (bf16[1280,256]{1,0:T(8,128)(2,1)}, bf16[12,16,1280]{2,1,0:T(8,128)(2,1)S(1)}) custom-call(s32[22]{0:T(128)S(1)} %broadcast_minimum_fusion.wave_ref, s32[22]{0:T(128)S(1)} %get-tuple-element.32.block_ref, bf16[4,1280,1280]{2,1,0:T(8,128)(2,1)} %table_ref.1, bf16[1280,512]{1,0:T(8,128)(2,1)} %bitcast.4.start_ref, f32[240,1280]{1,0:T(8,128)} %copy.72.skew_ref, ...), custom_call_target="tpu_custom_call" | custom-call | flops 44291850240 | bytes 7208960 | tf_op jit(solution)/shard_map/air_march/pallas_call | solution.py:355
  135.8 1.1 fusion.8
  137.8 4.8 %all-to-all-start.2 = ((bf16[32,16,256]{2,1,0:T(8,128)(2,1)}), bf16[32,16,256]{2,1,0:T(8,128)(2,1)S(1)}, u32[]{:S(2)}, u32[]{:S(2)}) async-start(bf16[32,16,256]{2,1,0:T(8,128)(2,1)} %bitcast.39), calls=%async_computation.2 | async-start | bytes 524288 | tf_op jit(solution)/shard_map/all_to_all | solution.py:390
  142.6 1.1 broadcast_select_fusion
  143.7 7.1 %all-to-all-done.2 = bf16[32,16,256]{2,1,0:T(8,128)(2,1)S(1)} async-done(((bf16[32,16,256]{2,1,0:T(8,128)(2,1)}), bf16[32,16,256]{2,1,0:T(8,128)(2,1)S(1)}, u32[]{:S(2)}, u32[]{:S(2)}) %all-to-all-start.2) | async-done | bytes 262176 | tf_op jit(solution)/shard_map/all_to_all | solution.py:390
  150.8 6.1 %all-to-all-start.1 = ((bf16[16,80,256]{2,1,0:T(8,128)(2,1)}), bf16[16,80,256]{2,1,0:T(8,128)(2,1)S(1)}, u32[]{:S(2)}, u32[]{:S(2)}) async-start(bf16[16,80,256]{2,1,0:T(8,128)(2,1)} %bitcast.31), calls=%async_computation.1 | async-start | bytes 1310720 | tf_op jit(solution)/shard_map/all_to_all | solution.py:399
  156.9 7.4 %ocean_march.1 = (f32[64,1440]{1,0:T(8,128)S(1)}, bf16[12,64,128]{2,1,0:T(8,128)(2,1)S(1)}) custom-call(f32[4,4]{1,0:T(4,128)S(1)} %bitcast_subtract_fusion.1.skew_ref, f32[64,1440]{1,0:T(8,128)S(1)} %bitcast.88, f32[64,1440]{1,0:T(8,128)S(1)} %bitcast.87, bf16[16,32,256]{2,1,0:T(8,128)(2,1)S(1)} %bitcast.89, bf16[128,1440]{1,0:T(8,128)(2,1)} %convert_element_type.77.basis_ref), custom_call_target="tpu_custom_call" | custom-call | flops 566231040 | bytes 1105920 | tf_op jit(solution)/shard_map/ocean_march/pallas_call | solution.py:414
  164.3 2.3 %collective-permute-start.2 = (bf16[12,2,16,128]{3,2,1,0:T(8,128)(2,1)S(1)}, bf16[12,2,16,128]{3,2,1,0:T(8,128)(2,1)S(1)}, u32[]{:S(2)}, u32[]{:S(2)}) collective-permute-start(bf16[12,2,16,128]{3,2,1,0:T(8,128)(2,1)S(1)} %get-tuple-element.22), channel_id=1, source_target_pairs={{2,0},{3,1},{4,2},{5,3},{6,4},{7,5},{8,6},{9,7},{10,8},{11,9},{12,... | collective-permute-start | bytes 294920 | tf_op jit(solution)/shard_map/ppermute | solution.py:452
  166.6 4.2 %collective-permute-start.3 = (bf16[12,2,16,128]{3,2,1,0:T(8,128)(2,1)S(1)}, bf16[12,2,16,128]{3,2,1,0:T(8,128)(2,1)S(1)}, u32[]{:S(2)}, u32[]{:S(2)}) collective-permute-start(bf16[12,2,16,128]{3,2,1,0:T(8,128)(2,1)S(1)} %get-tuple-element.22), channel_id=1, source_target_pairs={{0,2},{1,3},{2,4},{3,5},{4,6},{5,7},{6,8},{7,9},{8,10},{9,11},{10,... | collective-permute-start | bytes 294920 | tf_op jit(solution)/shard_map/ppermute | solution.py:452
  170.8 1.9 %collective-permute-start.4 = (bf16[12,2,16,128]{3,2,1,0:T(8,128)(2,1)S(1)}, bf16[12,2,16,128]{3,2,1,0:T(8,128)(2,1)S(1)}, u32[]{:S(2)}, u32[]{:S(2)}) collective-permute-start(bf16[12,2,16,128]{3,2,1,0:T(8,128)(2,1)S(1)} %get-tuple-element.21), channel_id=1, source_target_pairs={{2,1},{3,0},{4,3},{5,2},{6,5},{7,4},{8,7},{9,6},{10,9},{11,8},{12,... | collective-permute-start | bytes 294920 | tf_op jit(solution)/shard_map/ppermute | solution.py:452
  173.3 5.7 %collective-permute-start.6 = (bf16[12,2,16,128]{3,2,1,0:T(8,128)(2,1)S(1)}, bf16[12,2,16,128]{3,2,1,0:T(8,128)(2,1)S(1)}, u32[]{:S(2)}, u32[]{:S(2)}) collective-permute-start(bf16[12,2,16,128]{3,2,1,0:T(8,128)(2,1)S(1)} %get-tuple-element.21), channel_id=1, source_target_pairs={{0,3},{1,2},{2,5},{3,4},{4,7},{5,6},{6,9},{7,8},{8,11},{9,10},{10,... | collective-permute-start | bytes 294920 | tf_op jit(solution)/shard_map/ppermute | solution.py:452
  179.1 1.0 collective-permute-start.1
  180.7 1.3 convolution_bitcast_fusion
  182.0 2.9 %collective-permute-done.1 = f32[2,16,1440]{2,1,0:T(8,128)S(1)} collective-permute-done((f32[2,16,1440]{2,1,0:T(8,128)S(1)}, f32[2,16,1440]{2,1,0:T(8,128)S(1)}, u32[]{:S(2)}, u32[]{:S(2)}) %collective-permute-start.1) | collective-permute-done | bytes 184352 | tf_op jit(solution)/shard_map/ppermute | solution.py:253
  185.7 6.2 %unpack_rows.1 = f32[32,80,128]{2,1,0:T(8,128)} custom-call(bf16[16,80,256]{2,1,0:T(8,128)(2,1)S(1)} %all-to-all-done.1.in_ref), custom_call_target="tpu_custom_call" | custom-call | tf_op jit(solution)/shard_map/unpack_rows/pallas_call | solution.py:402
  (115 shorter events, 9.6 us)
Async XLA Ops:
  0.6 1.2 copy-start
  10.2 6.8 %copy-start.1 = (f32[2,32,1440]{2,1,0:T(8,128)S(1)}, f32[2,32,1440]{2,1,0:T(8,128)}, u32[]{:S(2)}) copy-start(f32[2,32,1440]{2,1,0:T(8,128)} %param.22) | copy-start | bytes 1105924
  10.2 6.8 %copy-start.2 = (f32[2,32,1440]{2,1,0:T(8,128)S(1)}, f32[2,32,1440]{2,1,0:T(8,128)}, u32[]{:S(2)}) copy-start(f32[2,32,1440]{2,1,0:T(8,128)} %param.23) | copy-start | bytes 1105924
  10.2 8.8 %copy-start.5 = (s32[64]{0:T(128)S(1)}, s32[64]{0:T(128)}, u32[]{:S(2)}) copy-start(s32[64]{0:T(128)} %param.18) | copy-start | bytes 772
  10.2 9.7 %copy-start.3 = (f32[2,16,16,80]{3,2,1,0:T(8,128)S(1)}, f32[2,16,16,80]{3,2,1,0:T(8,128)}, u32[]{:S(2)}) copy-start(f32[2,16,16,80]{3,2,1,0:T(8,128)} %param.19) | copy-start | bytes 491524
  10.2 57.5 %all-to-all-start = ((bf16[16,80,512]{2,1,0:T(8,128)(2,1)}), bf16[16,80,512]{2,1,0:T(8,128)(2,1)}, u32[]{:S(2)}, u32[]{:S(2)}) async-start(bf16[16,80,512]{2,1,0:T(8,128)(2,1)} %pack_rows.1), calls=%async_computation | async-start | bytes 2621440 | tf_op jit(solution)/shard_map/all_to_all | solution.py:308
  16.9 5.2 %copy-start.9 = (f32[32]{0:T(128)S(1)}, f32[32]{0:T(128)}, u32[]{:S(2)}) copy-start(f32[32]{0:T(128)} %param.27) | copy-start | bytes 388
  16.9 5.2 %copy-start.10 = (s32[32]{0:T(128)S(1)}, s32[32]{0:T(128)}, u32[]{:S(2)}) copy-start(s32[32]{0:T(128)} %param.26) | copy-start | bytes 388
  17.0 5.5 %copy-start.11 = (f32[80]{0:T(128)S(1)}, f32[80]{0:T(128)}, u32[]{:S(2)}) copy-start(f32[80]{0:T(128)} %param.16) | copy-start | bytes 964
  17.0 5.5 %copy-start.6 = (f32[2,80]{1,0:T(2,128)S(1)}, f32[2,80]{1,0:T(2,128)}, u32[]{:S(2)}) copy-start(f32[2,80]{1,0:T(2,128)} %param.20) | copy-start | bytes 1924
  17.8 124.8 %collective-permute-start = (f32[2,2,16,1440]{3,2,1,0:T(8,128)}, f32[2,2,16,1440]{3,2,1,0:T(8,128)}, u32[]{:S(2)}, u32[]{:S(2)}) collective-permute-start(f32[2,2,16,1440]{3,2,1,0:T(8,128)} %fusion.18), channel_id=1, source_target_pairs={{0,1},{1,0},{2,3},{3,2},{4,5},{5,4},{6,7},{7,6},{8,9},{9,8},{10,11... | collective-permute-start | bytes 1105928 | tf_op jit(solution)/shard_map/ppermute | solution.py:253
  64.3 2.2 %copy-start.4 = (f32[4,4]{1,0:T(4,128)S(1)}, f32[4,4]{1,0:T(4,128)}, u32[]{:S(2)}) copy-start(f32[4,4]{1,0:T(4,128)} %param.24) | copy-start | bytes 196
  64.5 2.9 %copy-start.8 = (f32[80]{0:T(128)S(1)}, f32[80]{0:T(128)}, u32[]{:S(2)}) copy-start(f32[80]{0:T(128)} %param.29) | copy-start | bytes 964
  64.5 2.9 %copy-start.7 = (s32[2,80]{1,0:T(2,128)S(1)}, s32[2,80]{1,0:T(2,128)}, u32[]{:S(2)}) copy-start(s32[2,80]{1,0:T(2,128)} %param.28) | copy-start | bytes 1924
  137.8 13.1 %all-to-all-start.2 = ((bf16[32,16,256]{2,1,0:T(8,128)(2,1)}), bf16[32,16,256]{2,1,0:T(8,128)(2,1)S(1)}, u32[]{:S(2)}, u32[]{:S(2)}) async-start(bf16[32,16,256]{2,1,0:T(8,128)(2,1)} %bitcast.39), calls=%async_computation.2 | async-start | bytes 524288 | tf_op jit(solution)/shard_map/all_to_all | solution.py:390
  150.8 34.9 %all-to-all-start.1 = ((bf16[16,80,256]{2,1,0:T(8,128)(2,1)}), bf16[16,80,256]{2,1,0:T(8,128)(2,1)S(1)}, u32[]{:S(2)}, u32[]{:S(2)}) async-start(bf16[16,80,256]{2,1,0:T(8,128)(2,1)} %bitcast.31), calls=%async_computation.1 | async-start | bytes 1310720 | tf_op jit(solution)/shard_map/all_to_all | solution.py:399
  164.3 14.7 %collective-permute-start.2 = (bf16[12,2,16,128]{3,2,1,0:T(8,128)(2,1)S(1)}, bf16[12,2,16,128]{3,2,1,0:T(8,128)(2,1)S(1)}, u32[]{:S(2)}, u32[]{:S(2)}) collective-permute-start(bf16[12,2,16,128]{3,2,1,0:T(8,128)(2,1)S(1)} %get-tuple-element.22), channel_id=1, source_target_pairs={{2,0},{3,1},{4,2},{5,3},{6,4},{7,5},{8,6},{9,7},{10,8},{11,9},{12,... | collective-permute-start | bytes 294920 | tf_op jit(solution)/shard_map/ppermute | solution.py:452
  166.6 13.5 %collective-permute-start.3 = (bf16[12,2,16,128]{3,2,1,0:T(8,128)(2,1)S(1)}, bf16[12,2,16,128]{3,2,1,0:T(8,128)(2,1)S(1)}, u32[]{:S(2)}, u32[]{:S(2)}) collective-permute-start(bf16[12,2,16,128]{3,2,1,0:T(8,128)(2,1)S(1)} %get-tuple-element.22), channel_id=1, source_target_pairs={{0,2},{1,3},{2,4},{3,5},{4,6},{5,7},{6,8},{7,9},{8,10},{9,11},{10,... | collective-permute-start | bytes 294920 | tf_op jit(solution)/shard_map/ppermute | solution.py:452
  170.8 9.3 %collective-permute-start.4 = (bf16[12,2,16,128]{3,2,1,0:T(8,128)(2,1)S(1)}, bf16[12,2,16,128]{3,2,1,0:T(8,128)(2,1)S(1)}, u32[]{:S(2)}, u32[]{:S(2)}) collective-permute-start(bf16[12,2,16,128]{3,2,1,0:T(8,128)(2,1)S(1)} %get-tuple-element.21), channel_id=1, source_target_pairs={{2,1},{3,0},{4,3},{5,2},{6,5},{7,4},{8,7},{9,6},{10,9},{11,8},{12,... | collective-permute-start | bytes 294920 | tf_op jit(solution)/shard_map/ppermute | solution.py:452
  172.7 7.5 %collective-permute-start.5 = (bf16[12,2,16,128]{3,2,1,0:T(8,128)(2,1)S(1)}, bf16[12,2,16,128]{3,2,1,0:T(8,128)(2,1)S(1)}, u32[]{:S(2)}, u32[]{:S(2)}) collective-permute-start(bf16[12,2,16,128]{3,2,1,0:T(8,128)(2,1)S(1)} %get-tuple-element.21), channel_id=1, source_target_pairs={{0,1},{1,0},{2,3},{3,2},{4,5},{5,4},{6,7},{7,6},{8,9},{9,8},{10,11... | collective-permute-start | bytes 294920 | tf_op jit(solution)/shard_map/ppermute | solution.py:452
  173.3 7.3 %collective-permute-start.6 = (bf16[12,2,16,128]{3,2,1,0:T(8,128)(2,1)S(1)}, bf16[12,2,16,128]{3,2,1,0:T(8,128)(2,1)S(1)}, u32[]{:S(2)}, u32[]{:S(2)}) collective-permute-start(bf16[12,2,16,128]{3,2,1,0:T(8,128)(2,1)S(1)} %get-tuple-element.21), channel_id=1, source_target_pairs={{0,3},{1,2},{2,5},{3,4},{4,7},{5,6},{6,9},{7,8},{8,11},{9,10},{10,... | collective-permute-start | bytes 294920 | tf_op jit(solution)/shard_map/ppermute | solution.py:452
  179.1 5.8 %collective-permute-start.1 = (f32[2,16,1440]{2,1,0:T(8,128)S(1)}, f32[2,16,1440]{2,1,0:T(8,128)S(1)}, u32[]{:S(2)}, u32[]{:S(2)}) collective-permute-start(f32[2,16,1440]{2,1,0:T(8,128)S(1)} %constant_dynamic-slice_fusion.2), channel_id=1, source_target_pairs={{0,1},{1,0},{2,3},{3,2},{4,5},{5,4},{6,7},{7,6},{8,9},{9,8},{10,11... | collective-permute-start | bytes 552968 | tf_op jit(solution)/shard_map/ppermute | solution.py:253
